TPU v7x, 1024 devices: a whole 4x8x16 slice. The times are simulated.
1024 devices in a mesh: node: 32 (over z, core), local: 32 (over x, y).
Axes of the slice: x: 4, y: 8, z: 16, core: 2. Of those that a mesh axis runs over, the one named last changes fastest.
Arguments:
- tokens: bfloat16 [131072, 7168], P(('node', 'local')), may hold values from -6 to 6
- route_cot: bfloat16 [12288, 7168], P(('node', 'local')), may hold values from -6 to 6
- expert_ids: int32 [131072, 8], P(('node', 'local')), may hold values from 0 to 255, all different within a row; in each aligned block of 128 rows (0 to 127, 128 to 255, ...) at most 6 rows name the same one
- w_gate: bfloat16 [2, 28672, 512], P(None, 'local'), may hold values from -0.0625 to 0.0625
- w_up: bfloat16 [2, 28672, 512], P(None, 'local'), may hold values from -0.0625 to 0.0625
- w_down: bfloat16 [2, 512, 28672], P(None, None, 'local'), may hold values from -0.125 to 0.125
Outputs:
- route_out: bfloat16 [12288, 7168], P(('node', 'local'))
- route_grad: bfloat16 [12288, 7168], P(('node', 'local'))
Inputs may be any that keep to these rules, and one draw needn't show every extreme that they name: `expert_ids`: each row names 8 different experts. Among the 128 tokens of one device no expert is named by more than 6 rows, a bound that some block reaches.
All inputs are finite; a program needn't handle non-finite values.
Results may differ from a plain program's by a relative error of at most 0.006.
Values may be sent and summed in bfloat16 or wider, within the bound.
No kernel may reach another device: no remote copies, remote signals or barrier semaphores. Data moves between devices by JAX's collectives and lax.ppermute only.
A program may use at most 32 MiB of HBM per device.

v0:
```python
import jax
import jax.numpy as jnp
from jax import lax
from jax.sharding import PartitionSpec as P

CAP = 6


def from_partner(value, axis, bit):
    mask = 2**bit
    pairs = [(source, source ^ mask) for source in range(lax.axis_size(axis))]
    return lax.ppermute(value, axis, pairs)


def silu_parts(values):
    logistic = jax.nn.sigmoid(values)
    return (values * logistic, logistic * (1.0 + values * (1.0 - logistic)))


def contract_last(left, right):
    return lax.dot_general(
        left, right, (((1,), (1,)), ((), ())), preferred_element_type=jnp.float32
    )


def partner_copy(values, bit):
    return from_partner(values, "local", bit)


def activations(summed):
    gate_pre = summed[:, 0, :]
    up_pre = summed[:, 1, :]
    hidden_grad = summed[:, 2, :]
    activation, slope = silu_parts(gate_pre)
    hidden = (activation * up_pre).astype(jnp.bfloat16)
    gate_delta = (hidden_grad * up_pre * slope).astype(jnp.bfloat16)
    up_delta = (hidden_grad * activation).astype(jnp.bfloat16)
    return jnp.stack([hidden, gate_delta, up_delta], axis=1)


def on_device(tokens, route_cot, expert_ids, w_gate, w_up, w_down):
    local_count = lax.axis_size("local")
    slice_count = min(8, local_count)
    block_count = local_count // slice_count
    slice_bits = slice_count.bit_length() - 1
    parity = lax.axis_index("node") % 2
    slice_index = lax.axis_index("local") % slice_count
    tok_count = tokens.shape[0]
    width = tokens.shape[1]
    slice_width = width // slice_count
    pair_count = 2 * CAP
    chosen = jnp.stack([expert_ids == 0, expert_ids == 1], axis=0)
    member = jnp.sum(chosen.astype(jnp.int32), axis=2)
    position = jnp.cumsum(member, axis=1) - member
    slot_iota = lax.broadcasted_iota(jnp.int32, (2, CAP, tok_count), 1)
    onehot = ((position[:, None, :] == slot_iota) & (member[:, None, :] == 1)).astype(jnp.bfloat16)
    packed_x = jnp.einsum("qct,td->qcd", onehot, tokens, preferred_element_type=jnp.float32).astype(
        jnp.bfloat16
    )
    packed_cot = route_cot.reshape(2, CAP, width)
    packed = jnp.stack([packed_x, packed_cot], axis=2)
    own_rows = lax.dynamic_index_in_dim(packed, parity, 0, keepdims=False)
    away_rows = lax.dynamic_index_in_dim(packed, 1 - parity, 0, keepdims=False)
    arrived = from_partner(away_rows, "node", 0)
    ordered = jnp.where(
        parity == 0,
        jnp.concatenate([own_rows, arrived], axis=0),
        jnp.concatenate([arrived, own_rows], axis=0),
    )
    pieces = ordered.reshape(pair_count, 2, slice_count, slice_width).transpose(2, 0, 1, 3)
    outgoing = jnp.tile(pieces, (block_count, 1, 1, 1))
    incoming = lax.all_to_all(outgoing, "local", split_axis=0, concat_axis=0, tiled=True)
    slot_rows = incoming.reshape(local_count * pair_count, 2, slice_width)
    slot_x = slot_rows[:, 0, :]
    slot_cot = slot_rows[:, 1, :]
    gate_slice = lax.dynamic_index_in_dim(w_gate, parity, 0, keepdims=False)
    up_slice = lax.dynamic_index_in_dim(w_up, parity, 0, keepdims=False)
    down_slice = lax.dynamic_index_in_dim(w_down, parity, 0, keepdims=False)
    partials = jnp.stack(
        [
            jnp.dot(slot_x, gate_slice, preferred_element_type=jnp.float32),
            jnp.dot(slot_x, up_slice, preferred_element_type=jnp.float32),
            contract_last(slot_cot, down_slice),
        ],
        axis=1,
    )
    share = partials
    for bit in range(slice_bits):
        half_rows = share.shape[0] // 2
        upper_kept = slice_index // (1 << bit) % 2 == 1
        lower = share[:half_rows]
        upper = share[half_rows:]
        kept = jnp.where(upper_kept, upper, lower)
        sent = jnp.where(upper_kept, lower, upper)
        share = kept + partner_copy(sent, bit)
    gathered = activations(share).astype(jnp.float32)
    for bit in reversed(range(slice_bits)):
        other = partner_copy(gathered, bit)
        upper_kept = slice_index // (1 << bit) % 2 == 1
        gathered = jnp.where(
            upper_kept,
            jnp.concatenate([other, gathered], axis=0),
            jnp.concatenate([gathered, other], axis=0),
        )
    expert_parts = gathered.astype(jnp.bfloat16)
    out_part = jnp.dot(
        expert_parts[:, 0, :], down_slice, preferred_element_type=jnp.float32
    ).astype(jnp.bfloat16)
    back_part = (
        contract_last(expert_parts[:, 1, :], gate_slice)
        + contract_last(expert_parts[:, 2, :], up_slice)
    ).astype(jnp.bfloat16)
    results = jnp.stack([out_part, back_part], axis=1).reshape(
        local_count, pair_count, 2, slice_width
    )
    returned = lax.all_to_all(results, "local", split_axis=0, concat_axis=0, tiled=True)
    blocks = jnp.sum(
        returned.reshape(block_count, slice_count, pair_count, 2, slice_width).astype(jnp.float32),
        axis=0,
    )
    combined = blocks.transpose(1, 2, 0, 3).reshape(pair_count, 2, width).astype(jnp.bfloat16)
    halves = combined.reshape(2, CAP, 2, width)
    own_back = lax.dynamic_index_in_dim(halves, parity, 0, keepdims=False)
    partner_part = lax.dynamic_index_in_dim(halves, 1 - parity, 0, keepdims=False)
    partner_back = from_partner(partner_part, "node", 0)
    by_expert = jnp.where(
        parity == 0, jnp.stack([own_back, partner_back]), jnp.stack([partner_back, own_back])
    )
    filled = jnp.sum(member, axis=1)
    valid = lax.broadcasted_iota(jnp.int32, (2, CAP), 1) < filled[:, None]
    zero = jnp.zeros((), jnp.bfloat16)
    route_out = jnp.where(valid[:, :, None], by_expert[:, :, 0, :], zero).reshape(pair_count, width)
    route_grad = jnp.where(valid[:, :, None], by_expert[:, :, 1, :], zero).reshape(
        pair_count, width
    )
    return (route_out, route_grad)


def solution(mesh):
    return jax.shard_map(
        on_device,
        mesh=mesh,
        in_specs=(
            P(("node", "local"), None),
            P(("node", "local"), None),
            P(("node", "local"), None),
            P(None, "local", None),
            P(None, "local", None),
            P(None, None, "local"),
        ),
        out_specs=(P(("node", "local"), None), P(("node", "local"), None)),
        check_vma=False,
    )
```

profile of v0, /device:TPU:1, one launch (start us, length us, event | category | flops | bytes accessed | tf_op | source)
XLA Modules:
  0.0 261.1 jit_solution(11072930190018168498)
XLA Ops:
  0.7 0.8 compare_bitcast_fusion.1
  1.5 0.6 convert_reduce_fusion.1
  2.1 0.3 reduce_window_sum.11
  2.4 1.0 stack_reshape.3
  3.5 1.8 fusion
  5.6 16.1 %collective-permute-start = (bf16[6,2,7168]{2,1,0:T(2,128)(2,1)S(1)}, bf16[6,2,7168]{2,1,0:T(2,128)(2,1)S(1)}, u32[]{:S(2)}, u32[]{:S(2)}) collective-permute-start(bf16[6,2,7168]{2,1,0:T(2,128)(2,1)S(1)} %bitcast.71), channel_id=1, source_target_pairs={{0,32},{32,0},{64,96},{96,64},{128,160},{160,128},{192,224},{224,1... | collective-permute-start | bytes 516104 | tf_op jit(solution)/shard_map/ppermute | solution.py:12
  21.9 0.8 collective-permute-done
  22.9 0.3 copy.18
  23.2 1.8 tile.4
  25.0 4.0 %all-to-all-start = ((bf16[32,12,2,896]{3,2,1,0:T(2,128)(2,1)}), bf16[32,12,2,896]{3,2,1,0:T(2,128)(2,1)S(1)}, u32[]{:S(2)}, u32[]{:S(2)}) async-start(bf16[32,12,2,896]{3,2,1,0:T(2,128)(2,1)} %bitcast.67), calls=%async_computation | async-start | bytes 2752512 | tf_op jit(solution)/shard_map/all_to_all | solution.py:72
  29.0 33.0 %all-to-all-done = bf16[32,12,2,896]{3,2,1,0:T(2,128)(2,1)S(1)} async-done(((bf16[32,12,2,896]{3,2,1,0:T(2,128)(2,1)}), bf16[32,12,2,896]{3,2,1,0:T(2,128)(2,1)S(1)}, u32[]{:S(2)}, u32[]{:S(2)}) %all-to-all-start) | async-done | bytes 1376288 | tf_op jit(solution)/shard_map/all_to_all | solution.py:72
  62.0 1.9 fusion.37
  63.9 0.6 convolution_bitcast_fusion.1
  64.5 0.9 copy-done.6
  65.4 0.6 convolution_bitcast_fusion.2
  66.0 0.6 convolution_bitcast_fusion
  67.1 1.2 copy-done.1
  68.2 5.6 %collective-permute-start.1 = (f32[192,3,512]{2,0,1:T(8,128)S(1)}, f32[192,3,512]{2,0,1:T(8,128)}, u32[]{:S(2)}, u32[]{:S(2)}) collective-permute-start(f32[192,3,512]{2,0,1:T(8,128)S(1)} %slice_select_fusion), channel_id=1, source_target_pairs={{0,1},{1,0},{2,3},{3,2},{4,5},{5,4},{6,7},{7,6},{8,9},{9,8},{10,11... | collective-permute-start | bytes 3538952 | tf_op jit(solution)/shard_map/ppermute | solution.py:12
  73.9 25.0 %collective-permute-done.1 = f32[192,3,512]{2,0,1:T(8,128)} collective-permute-done((f32[192,3,512]{2,0,1:T(8,128)S(1)}, f32[192,3,512]{2,0,1:T(8,128)}, u32[]{:S(2)}, u32[]{:S(2)}) %collective-permute-start.1) | collective-permute-done | bytes 1179680 | tf_op jit(solution)/shard_map/ppermute | solution.py:12
  98.9 2.4 select_add_fusion
  101.3 0.9 slice_select_fusion.1
  102.2 1.9 collective-permute-start.2
  104.2 27.3 %collective-permute-done.2 = f32[96,3,512]{2,0,1:T(8,128)} collective-permute-done((f32[96,3,512]{2,0,1:T(8,128)}, f32[96,3,512]{2,0,1:T(8,128)}, u32[]{:S(2)}, u32[]{:S(2)}) %collective-permute-start.2) | collective-permute-done | bytes 589856 | tf_op jit(solution)/shard_map/ppermute | solution.py:12
  131.5 1.2 select_add_fusion.1
  132.8 5.4 %collective-permute-start.3 = (f32[48,3,512]{2,0,1:T(8,128)S(1)}, f32[48,3,512]{2,0,1:T(8,128)S(1)}, u32[]{:S(2)}, u32[]{:S(2)}) collective-permute-start(f32[48,3,512]{2,0,1:T(8,128)S(1)} %slice_select_fusion.2), channel_id=1, source_target_pairs={{0,4},{1,5},{2,6},{3,7},{4,0},{5,1},{6,2},{7,3},{8,12},{9,13},{10,... | collective-permute-start | bytes 884744 | tf_op jit(solution)/shard_map/ppermute | solution.py:12
  138.2 15.2 %collective-permute-done.3 = f32[48,3,512]{2,0,1:T(8,128)S(1)} collective-permute-done((f32[48,3,512]{2,0,1:T(8,128)S(1)}, f32[48,3,512]{2,0,1:T(8,128)S(1)}, u32[]{:S(2)}, u32[]{:S(2)}) %collective-permute-start.3) | collective-permute-done | bytes 294944 | tf_op jit(solution)/shard_map/ppermute | solution.py:12
  153.5 4.6 %collective-permute-start.4 = (bf16[48,3,512]{2,0,1:T(8,128)(2,1)S(1)}, bf16[48,3,512]{2,0,1:T(8,128)(2,1)S(1)}, u32[]{:S(2)}, u32[]{:S(2)}) collective-permute-start(bf16[48,3,512]{2,0,1:T(8,128)(2,1)S(1)} %maximum_convert_fusion), channel_id=1, source_target_pairs={{0,4},{1,5},{2,6},{3,7},{4,0},{5,1},{6,2},{7,3},{8,12},{9,13},{10,... | collective-permute-start | bytes 442376 | tf_op jit(solution)/shard_map/ppermute | solution.py:12
  158.2 5.1 %collective-permute-done.4 = bf16[48,3,512]{2,0,1:T(8,128)(2,1)S(1)} collective-permute-done((bf16[48,3,512]{2,0,1:T(8,128)(2,1)S(1)}, bf16[48,3,512]{2,0,1:T(8,128)(2,1)S(1)}, u32[]{:S(2)}, u32[]{:S(2)}) %collective-permute-start.4) | collective-permute-done | bytes 147488 | tf_op jit(solution)/shard_map/ppermute | solution.py:12
  163.4 1.9 collective-permute-start.5
  165.3 16.0 %collective-permute-done.5 = bf16[96,3,512]{2,0,1:T(8,128)(2,1)S(1)} collective-permute-done((bf16[96,3,512]{2,0,1:T(8,128)(2,1)S(1)}, bf16[96,3,512]{2,0,1:T(8,128)(2,1)S(1)}, u32[]{:S(2)}, u32[]{:S(2)}) %collective-permute-start.5) | collective-permute-done | bytes 294944 | tf_op jit(solution)/shard_map/ppermute | solution.py:12
  181.6 2.1 collective-permute-start.6
  183.7 14.1 %collective-permute-done.6 = bf16[192,3,512]{2,0,1:T(8,128)(2,1)S(1)} collective-permute-done((bf16[192,3,512]{2,0,1:T(8,128)(2,1)S(1)}, bf16[192,3,512]{2,0,1:T(8,128)(2,1)S(1)}, u32[]{:S(2)}, u32[]{:S(2)}) %collective-permute-start.6) | collective-permute-done | bytes 589856 | tf_op jit(solution)/shard_map/ppermute | solution.py:12
  197.8 0.5 fusion.1
  198.3 1.4 convolution_convert_fusion.1
  199.8 0.7 copy-done.5
  200.5 0.6 fusion.6
  201.1 2.1 stack.64
  203.2 2.8 %fusion.3 = bf16[384,896]{1,0:T(8,128)(2,1)} fusion(f32[384,896]{1,0:T(8,128)S(1)} %fusion.6, bf16[2,896,512]{2,1,0:T(8,128)(2,1)} %param.9, s32[]{:T(128)S(6)} %select_n.151, bf16[384,3,512]{2,0,1:T(8,128)(2,1)} %copy-done.3), kind=kOutput, calls=%fused_computation.8 | convolution fusion | flops 353009664 | bytes 3375108 | tf_op jit(solution)/shard_map/dot_general | solution.py:21
  206.0 2.2 stack.65
  208.2 1.5 pad_maximum_fusion.1
  209.7 1.4 copy.19
  211.1 36.7 %all_to_all.10 = bf16[32,12,2,896]{3,2,1,0:T(2,128)(2,1)S(1)} all-to-all(bf16[32,12,2,896]{3,2,1,0:T(2,128)(2,1)S(1)} %copy.19), channel_id=1, replica_groups=mesh['node'=32,'local'=32] {'local'}, dimensions={0} | all-to-all | bytes 2752512 | tf_op jit(solution)/shard_map/all_to_all | solution.py:116
  247.8 1.9 reduce.1
  250.1 7.0 %collective-permute-start.7 = (bf16[6,2,7168]{2,1,0:T(2,128)(2,1)S(1)}, bf16[6,2,7168]{2,1,0:T(2,128)(2,1)S(1)}, u32[]{:S(2)}, u32[]{:S(2)}) collective-permute-start(bf16[6,2,7168]{2,1,0:T(2,128)(2,1)S(1)} %get-tuple-element.11), channel_id=1, source_target_pairs={{0,32},{32,0},{64,96},{96,64},{128,160},{160,128},{192,224},{224,1... | collective-permute-start | bytes 516104 | tf_op jit(solution)/shard_map/ppermute | solution.py:12
  257.3 0.8 collective-permute-done.7
  258.1 0.5 broadcast_select_fusion
  258.6 1.4 slice_reduce_fusion
  260.2 0.9 broadcast_select_fusion.1
  (35 shorter events, 2.3 us)
Async XLA Ops:
  0.6 65.4 %copy-start = (bf16[2,512,896]{2,1,0:T(8,128)(2,1)S(1)}, bf16[2,512,896]{2,1,0:T(8,128)(2,1)}, u32[]{:S(2)}) copy-start(bf16[2,512,896]{2,1,0:T(8,128)(2,1)} %param.11) | copy-start | bytes 5505028
  5.6 17.1 %collective-permute-start = (bf16[6,2,7168]{2,1,0:T(2,128)(2,1)S(1)}, bf16[6,2,7168]{2,1,0:T(2,128)(2,1)S(1)}, u32[]{:S(2)}, u32[]{:S(2)}) collective-permute-start(bf16[6,2,7168]{2,1,0:T(2,128)(2,1)S(1)} %bitcast.71), channel_id=1, source_target_pairs={{0,32},{32,0},{64,96},{96,64},{128,160},{160,128},{192,224},{224,1... | collective-permute-start | bytes 516104 | tf_op jit(solution)/shard_map/ppermute | solution.py:12
  25.0 37.0 %all-to-all-start = ((bf16[32,12,2,896]{3,2,1,0:T(2,128)(2,1)}), bf16[32,12,2,896]{3,2,1,0:T(2,128)(2,1)S(1)}, u32[]{:S(2)}, u32[]{:S(2)}) async-start(bf16[32,12,2,896]{3,2,1,0:T(2,128)(2,1)} %bitcast.67), calls=%async_computation | async-start | bytes 2752512 | tf_op jit(solution)/shard_map/all_to_all | solution.py:72
  62.0 1.9 copy-start.4
  63.9 1.5 copy-start.6
  66.8 1.4 copy-start.1
  68.2 30.6 %collective-permute-start.1 = (f32[192,3,512]{2,0,1:T(8,128)S(1)}, f32[192,3,512]{2,0,1:T(8,128)}, u32[]{:S(2)}, u32[]{:S(2)}) collective-permute-start(f32[192,3,512]{2,0,1:T(8,128)S(1)} %slice_select_fusion), channel_id=1, source_target_pairs={{0,1},{1,0},{2,3},{3,2},{4,5},{5,4},{6,7},{7,6},{8,9},{9,8},{10,11... | collective-permute-start | bytes 3538952 | tf_op jit(solution)/shard_map/ppermute | solution.py:12
  102.2 29.3 %collective-permute-start.2 = (f32[96,3,512]{2,0,1:T(8,128)}, f32[96,3,512]{2,0,1:T(8,128)}, u32[]{:S(2)}, u32[]{:S(2)}) collective-permute-start(f32[96,3,512]{2,0,1:T(8,128)} %slice_select_fusion.1), channel_id=1, source_target_pairs={{0,2},{1,3},{2,0},{3,1},{4,6},{5,7},{6,4},{7,5},{8,10},{9,11},{10,... | collective-permute-start | bytes 1769480 | tf_op jit(solution)/shard_map/ppermute | solution.py:12
  132.8 20.6 %collective-permute-start.3 = (f32[48,3,512]{2,0,1:T(8,128)S(1)}, f32[48,3,512]{2,0,1:T(8,128)S(1)}, u32[]{:S(2)}, u32[]{:S(2)}) collective-permute-start(f32[48,3,512]{2,0,1:T(8,128)S(1)} %slice_select_fusion.2), channel_id=1, source_target_pairs={{0,4},{1,5},{2,6},{3,7},{4,0},{5,1},{6,2},{7,3},{8,12},{9,13},{10,... | collective-permute-start | bytes 884744 | tf_op jit(solution)/shard_map/ppermute | solution.py:12
  153.5 9.8 %collective-permute-start.4 = (bf16[48,3,512]{2,0,1:T(8,128)(2,1)S(1)}, bf16[48,3,512]{2,0,1:T(8,128)(2,1)S(1)}, u32[]{:S(2)}, u32[]{:S(2)}) collective-permute-start(bf16[48,3,512]{2,0,1:T(8,128)(2,1)S(1)} %maximum_convert_fusion), channel_id=1, source_target_pairs={{0,4},{1,5},{2,6},{3,7},{4,0},{5,1},{6,2},{7,3},{8,12},{9,13},{10,... | collective-permute-start | bytes 442376 | tf_op jit(solution)/shard_map/ppermute | solution.py:12
  163.4 18.0 %collective-permute-start.5 = (bf16[96,3,512]{2,0,1:T(8,128)(2,1)S(1)}, bf16[96,3,512]{2,0,1:T(8,128)(2,1)S(1)}, u32[]{:S(2)}, u32[]{:S(2)}) collective-permute-start(bf16[96,3,512]{2,0,1:T(8,128)(2,1)S(1)} %maximum_select_fusion.2), channel_id=1, source_target_pairs={{0,2},{1,3},{2,0},{3,1},{4,6},{5,7},{6,4},{7,5},{8,10},{9,11},{10,... | collective-permute-start | bytes 884744 | tf_op jit(solution)/shard_map/ppermute | solution.py:12
  181.6 16.2 %collective-permute-start.6 = (bf16[192,3,512]{2,0,1:T(8,128)(2,1)S(1)}, bf16[192,3,512]{2,0,1:T(8,128)(2,1)S(1)}, u32[]{:S(2)}, u32[]{:S(2)}) collective-permute-start(bf16[192,3,512]{2,0,1:T(8,128)(2,1)S(1)} %maximum_select_fusion.1), channel_id=1, source_target_pairs={{0,1},{1,0},{2,3},{3,2},{4,5},{5,4},{6,7},{7,6},{8,9},{9,8},{10,11... | collective-permute-start | bytes 1769480 | tf_op jit(solution)/shard_map/ppermute | solution.py:12
  198.3 1.5 copy-start.3
  198.3 2.2 copy-start.5
  206.0 2.2 copy-start.2
  249.7 7.4 %copy-start.7 = (s32[2]{0:T(128)S(1)}, s32[2]{0:T(128)}, u32[]{:S(2)}) copy-start(s32[2]{0:T(128)} %get-tuple-element.4) | copy-start | bytes 28
  250.1 8.0 %collective-permute-start.7 = (bf16[6,2,7168]{2,1,0:T(2,128)(2,1)S(1)}, bf16[6,2,7168]{2,1,0:T(2,128)(2,1)S(1)}, u32[]{:S(2)}, u32[]{:S(2)}) collective-permute-start(bf16[6,2,7168]{2,1,0:T(2,128)(2,1)S(1)} %get-tuple-element.11), channel_id=1, source_target_pairs={{0,32},{32,0},{64,96},{96,64},{128,160},{160,128},{192,224},{224,1... | collective-permute-start | bytes 516104 | tf_op jit(solution)/shard_map/ppermute | solution.py:12
where the time goes:
time: 262 us; the launch traced here: 261 us
  waiting for transfers between devices  137 us (52%)
  starting transfers between devices  48.5 us (19%)
  blocking collectives  36.7 us (14%)
  local copies, waits for them, and re-layouts  16 us (6%)
  other arithmetic  12.9 us (5%)
  matrix products  8.41 us (3%)
    ppermute x8, waiting for transfers between devices, from_partner(): return lax.ppermute(value, axis, pairs)  104 us
    ppermute x8, starting transfers between devices, from_partner(): return lax.ppermute(value, axis, pairs)  44.6 us
    all_to_all x1, blocking collectives, on_device(): lax.all_to_all(results, 'local', split_axis=0, concat_axis=0, tiled=True)  36.7 us
    all_to_all x1, waiting for transfers between devices, on_device(): lax.all_to_all(outgoing, 'local', split_axis=0, concat_axis=0, tiled=True)  33 us
    another operation x3, local copies, waits for them, and re-layouts, on_device(): jnp.stack([out_part, back_part], axis=1)  5.69 us
  transfers between devices with their start and end apart: 9, of which 9 were waited for; matrix products, arithmetic and copies ran while one was open for 0% of the time, Pallas kernels for 0%

commit v1 on v0

v1 whole, which is shorter than its diff:
```python
import jax
import jax.numpy as jnp
import numpy as np
from jax import lax
from jax.experimental import pallas as pl
from jax.experimental.pallas import tpu as pltpu
from jax.sharding import Mesh, PartitionSpec as P

CAP = 6
XS = 4
YS = 8
SLOTS = 2 * CAP
ROWS = 2 * SLOTS
BF16 = jnp.bfloat16
F32 = jnp.float32


def dot_nn(left, right):
    return jnp.dot(left, right, preferred_element_type=F32)


def dot_nt(left, right):
    return lax.dot_general(
        left, right, (((1,), (1,)), ((), ())), preferred_element_type=F32
    )


def regroup():
    index = np.arange(YS * ROWS).reshape(YS, 2, 2, CAP).transpose(1, 2, 0, 3).reshape(-1)
    return np.eye(YS * ROWS, dtype=np.float32)[index]


def slot_onehot(ids_t, rows):
    count = ids_t.shape[1]
    row = lax.broadcasted_iota(jnp.int32, (rows, count), 0)
    first = row < CAP
    named = [
        jnp.max(jnp.where(ids_t == q, 1.0, 0.0), axis=0, keepdims=True) for q in range(2)
    ]
    member = jnp.where(first, named[0], named[1])
    before = (
        lax.broadcasted_iota(jnp.int32, (count, count), 0)
        < lax.broadcasted_iota(jnp.int32, (count, count), 1)
    )
    position = dot_nn(member.astype(BF16), jnp.where(before, 1.0, 0.0).astype(BF16))
    wanted = jnp.where(first, row, row - CAP).astype(F32)
    hit = (position == wanted) & (member > 0.5) & (row < SLOTS)
    return jnp.where(hit, 1.0, 0.0)


def pack_kernel(ids_ref, tok_ref, cot_ref, out_ref):
    onehot = slot_onehot(ids_ref[...], ROWS).astype(BF16)
    lift = (
        lax.broadcasted_iota(jnp.int32, (ROWS, SLOTS), 0)
        == lax.broadcasted_iota(jnp.int32, (ROWS, SLOTS), 1) + SLOTS
    )
    lift = jnp.where(lift, 1.0, 0.0).astype(BF16)
    width = out_ref.shape[2]
    for s in range(YS):
        cols = slice(s * width, (s + 1) * width)
        out_ref[s] = (
            dot_nn(onehot, tok_ref[:, cols]) + dot_nn(lift, cot_ref[:, cols])
        ).astype(BF16)


def first_kernel(perm_ref, rows_ref, wg_ref, wu_ref, wd_ref, out_ref, lhs_ref):
    block = YS * CAP
    for xs in range(XS):
        moved = dot_nn(perm_ref[...], rows_ref[xs]).astype(BF16)
        for j in range(4):
            lhs_ref[j, pl.ds(xs * block, block), :] = moved[j * block : (j + 1) * block]
    for q in range(2):
        x = lhs_ref[q]
        cot = lhs_ref[2 + q]
        parts = (dot_nn(x, wg_ref[q]), dot_nn(x, wu_ref[q]), dot_nt(cot, wd_ref[q]))
        for j, part in enumerate(parts):
            hidden = part.shape[1]
            out_ref[q * XS : (q + 1) * XS, :, j * hidden : (j + 1) * hidden] = part.astype(
                BF16
            ).reshape(XS, block, hidden)


def act_kernel(sum_ref, out_ref):
    hidden = out_ref.shape[1] // 3

    def total(j):
        cols = slice(j * hidden, (j + 1) * hidden)
        value = sum_ref[0, :, cols].astype(F32)
        for s in range(1, YS):
            value = value + sum_ref[s, :, cols].astype(F32)
        return value

    gate, up, grad = total(0), total(1), total(2)
    logistic = jax.nn.sigmoid(gate)
    activation = gate * logistic
    slope = logistic * (1.0 + gate * (1.0 - logistic))
    out_ref[:, :hidden] = (activation * up).astype(BF16)
    out_ref[:, hidden : 2 * hidden] = (grad * up * slope).astype(BF16)
    out_ref[:, 2 * hidden :] = (grad * activation).astype(BF16)


def second_kernel(back_ref, act_ref, wg_ref, wu_ref, wd_ref, out_ref, res_ref):
    block = YS * CAP
    hidden = act_ref.shape[2] // 3
    for q in range(2):
        mine = act_ref[q * XS : (q + 1) * XS].reshape(XS * block, 3 * hidden)
        out = dot_nn(mine[:, :hidden], wd_ref[q])
        grad = dot_nt(mine[:, hidden : 2 * hidden], wg_ref[q]) + dot_nt(
            mine[:, 2 * hidden :], wu_ref[q]
        )
        for kind, part in enumerate((out, grad)):
            start = (kind * 2 + q) * block
            res_ref[:, pl.ds(start, block), :] = part.astype(BF16).reshape(
                XS, block, part.shape[1]
            )
    for xs in range(XS):
        out_ref[xs] = dot_nn(back_ref[...], res_ref[xs]).astype(BF16)


def sum_kernel(parts_ref, out_ref):
    total = parts_ref[0].astype(F32)
    for i in range(1, XS):
        total = total + parts_ref[i].astype(F32)
    out_ref[...] = total.astype(BF16)


def final_kernel(ids_ref, rows_ref, out_ref, grad_ref):
    valid = jnp.sum(slot_onehot(ids_ref[...], SLOTS), axis=1, keepdims=True) > 0.5
    width = rows_ref.shape[2]
    row = lax.broadcasted_iota(jnp.int32, (SLOTS, ROWS), 0)
    col = lax.broadcasted_iota(jnp.int32, (SLOTS, ROWS), 1)
    pick_out = jnp.where((row == col) & valid, 1.0, 0.0).astype(BF16)
    pick_grad = jnp.where((row + SLOTS == col) & valid, 1.0, 0.0).astype(BF16)
    for s in range(YS):
        cols = slice(s * width, (s + 1) * width)
        out_ref[:, cols] = dot_nn(pick_out, rows_ref[s]).astype(BF16)
        grad_ref[:, cols] = dot_nn(pick_grad, rows_ref[s]).astype(BF16)


def call(kernel, outs, scratch=(), vmem=48):
    spec = pl.BlockSpec(memory_space=pltpu.VMEM)
    single = not isinstance(outs, (tuple, list))

    def run(*args):
        return pl.pallas_call(
            kernel,
            out_shape=outs,
            in_specs=[spec] * len(args),
            out_specs=spec if single else tuple(spec for _ in outs),
            scratch_shapes=list(scratch),
            compiler_params=pltpu.CompilerParams(vmem_limit_bytes=vmem * 1024 * 1024),
        )(*args)

    return run


def on_device(tokens, route_cot, expert_ids, w_gate, w_up, w_down):
    width = tokens.shape[1]
    part = width // YS
    hidden = w_gate.shape[2]
    block = YS * CAP
    ids_t = expert_ids.T
    perm = jnp.asarray(regroup(), BF16)
    back = jnp.asarray(regroup().T, BF16)
    shape = jax.ShapeDtypeStruct

    packed = call(pack_kernel, shape((YS, ROWS, part), BF16))(ids_t, tokens, route_cot)
    sliced = lax.all_to_all(packed, "y", split_axis=0, concat_axis=0, tiled=True)
    rows = lax.all_gather(sliced, "x", axis=0, tiled=False).reshape(XS, YS * ROWS, part)
    partials = call(
        first_kernel,
        shape((2 * XS, block, 3 * hidden), BF16),
        [pltpu.VMEM((4, XS * block, part), BF16)],
    )(perm, rows, w_gate, w_up, w_down)
    shares = lax.all_to_all(partials, "y", split_axis=0, concat_axis=0, tiled=True)
    acts = call(act_kernel, shape((block, 3 * hidden), BF16))(shares)
    gathered = lax.all_gather(acts, "y", axis=0, tiled=False)
    results = call(
        second_kernel,
        shape((XS, YS * ROWS, part), BF16),
        [pltpu.VMEM((XS, YS * ROWS, part), BF16)],
    )(back, gathered, w_gate, w_up, w_down)
    blocks = lax.all_to_all(results, "x", split_axis=0, concat_axis=0, tiled=True)
    total = call(sum_kernel, shape((YS * ROWS, part), BF16))(blocks)
    home = lax.all_to_all(
        total.reshape(YS, ROWS, part), "y", split_axis=0, concat_axis=0, tiled=True
    )
    return call(final_kernel, (shape((SLOTS, width), BF16),) * 2)(ids_t, home)


def solution(mesh):
    nodes = mesh.devices.shape[0]
    grid = Mesh(mesh.devices.reshape(nodes, XS, YS), ("node", "x", "y"))
    rows = P(("node", "x", "y"), None)
    return jax.shard_map(
        on_device,
        mesh=grid,
        in_specs=(
            rows,
            rows,
            rows,
            P(None, ("x", "y"), None),
            P(None, ("x", "y"), None),
            P(None, None, ("x", "y")),
        ),
        out_specs=(rows, rows),
        check_vma=False,
    )
```

time: 262 us -> 205 us (0.78)
  the two profiles are of different devices: /device:TPU:1 before, /device:TPU:64 now
where the time goes in v1:
time: 205 us; the launch traced here: 204 us
  blocking collectives  92.5 us (45%)
  waiting for transfers between devices  80.5 us (39%)
  between operations  14.1 us (7%)
  Pallas kernels  11.2 us (5%)
  local copies, waits for them, and re-layouts  5.74 us (3%)
    all_gather x1, waiting for transfers between devices, on_device(): gathered = lax.all_gather(acts, 'y', axis=0, tiled=False)  42.8 us
    all_gather x1, waiting for transfers between devices, on_device(): lax.all_gather(sliced, 'x', axis=0, tiled=False)  37.7 us
    all_to_all x1, blocking collectives, on_device(): lax.all_to_all(partials, 'y', split_axis=0, concat_axis=0, tiled=True)  37.5 us
    all_to_all x1, blocking collectives, on_device(): lax.all_to_all(packed, 'y', split_axis=0, concat_axis=0, tiled=True)  20.6 us
    all_to_all x1, blocking collectives, on_device(): lax.all_to_all(results, 'x', split_axis=0, concat_axis=0, tiled=True)  18.5 us
    all_to_all x1, blocking collectives, on_device(): lax.all_to_all(total.reshape(YS, ROWS, part), 'y', split_axis=0, concat_a...  15.9 us
    pallas_call x6, Pallas kernels, run(): pl.pallas_call(kernel, out_shape=outs, in_specs=[spec] * len(args), out_s...  11.2 us
    unnamed x18, local copies, waits for them, and re-layouts  5.74 us
  transfers between devices with their start and end apart: 2, of which 2 were waited for; matrix products, arithmetic and copies ran while one was open for 0% of the time, Pallas kernels for 0%

profile of v1, /device:TPU:64, one launch (start us, length us, event | category | flops | bytes accessed | tf_op | source)
XLA Modules:
  0.0 204.1 jit_solution(17579036118653662033)
XLA Ops:
  7.2 0.0 all-gather.5.cloned.1.call-start
  7.2 0.0 copy-start.1
  7.2 1.5 copy-done.1
  8.7 0.0 copy-start.4
  8.7 0.9 copy-done.4
  9.7 0.0 copy-start.7
  9.7 0.7 copy-done.7
  10.3 0.0 copy-start
  10.3 0.0 copy-start.6
  10.3 0.6 shard_map.95
  11.0 20.6 %all_to_all.20 = bf16[8,24,896]{2,1,0:T(8,128)(2,1)} all-to-all(bf16[8,24,896]{2,1,0:T(8,128)(2,1)S(1)} %shard_map.95), channel_id=1, replica_groups=mesh['node'=32,'x'=4,'y'=8] {'y'}, dimensions={0} | all-to-all | bytes 688128 | tf_op jit(solution)/shard_map/all_to_all | solution.py:168
  31.6 0.0 all-gather.5.cloned.1.call-update
  31.6 0.0 all-gather.7.cloned.1.call-start
  31.7 37.7 %all-gather.5.cloned.1.call-done = bf16[32,24,896]{2,1,0:T(8,128)(2,1)} async-done(((bf16[8,24,896]{2,1,0:T(8,128)(2,1)}), bf16[32,24,896]{2,1,0:T(8,128)(2,1)}) %all-gather.5.cloned.1.call-update) | async-done | bytes 1376272 | tf_op jit(solution)/shard_map/all_gather | solution.py:169
  69.4 0.0 copy-done
  69.4 0.0 copy-done.6
  69.4 0.0 copy-start.2
  69.4 1.3 copy-done.2
  70.7 4.0 %shard_map.96 = bf16[8,48,1536]{2,1,0:T(8,128)(2,1)S(1)} custom-call(bf16[192,192]{1,0:T(8,128)(2,1)S(1)} %copy-done.6, bf16[4,192,896]{2,1,0:T(8,128)(2,1)S(1)} %bitcast.5, bf16[2,896,512]{2,1,0:T(8,128)(2,1)S(1)} %copy-done, bf16[2,896,512]{2,1,0:T(8,128)(2,1)} %wu_ref.3, bf16[2,512,896]{2,1,0:T(8,128)(2,1)} %wd_ref.3), custom_call_target="tpu_custom_call" | custom-call | tf_op jit(solution)/shard_map/pallas_call | solution.py:145
  74.8 0.0 copy-start.5
  74.8 37.5 %all_to_all.21.sum_ref = bf16[8,48,1536]{2,1,0:T(8,128)(2,1)S(1)} all-to-all(bf16[8,48,1536]{2,1,0:T(8,128)(2,1)S(1)} %shard_map.96), channel_id=1, replica_groups=mesh['node'=32,'x'=4,'y'=8] {'y'}, dimensions={0} | all-to-all | bytes 2359296 | tf_op jit(solution)/shard_map/all_to_all | solution.py:175
  112.3 0.9 shard_map.97
  113.1 0.0 all-gather.7.cloned.1.call-update
  113.1 42.8 %all-gather.7.cloned.1.call-done = bf16[384,1536]{1,0:T(8,128)(2,1)} async-done(((bf16[48,1536]{1,0:T(8,128)(2,1)}), bf16[384,1536]{1,0:T(8,128)(2,1)}) %all-gather.7.cloned.1.call-update) | async-done | bytes 1179664 | tf_op jit(solution)/shard_map/all_gather | solution.py:177
  155.9 0.0 copy-done.5
  155.9 0.0 copy-start.3
  155.9 1.3 copy-done.3
  157.2 4.2 %shard_map.98 = bf16[4,192,896]{2,1,0:T(8,128)(2,1)S(1)} custom-call(bf16[192,192]{1,0:T(8,128)(2,1)S(1)} %copy-done.5, bf16[8,48,1536]{2,1,0:T(8,128)(2,1)S(1)} %bitcast.6, bf16[2,896,512]{2,1,0:T(8,128)(2,1)S(1)} %copy-done, bf16[2,896,512]{2,1,0:T(8,128)(2,1)} %wu_ref.3, bf16[2,512,896]{2,1,0:T(8,128)(2,1)} %wd_ref.3), custom_call_target="tpu_custom_call" | custom-call | tf_op jit(solution)/shard_map/pallas_call | solution.py:145
  161.4 18.5 %all_to_all.22.parts_ref = bf16[4,192,896]{2,1,0:T(8,128)(2,1)S(1)} all-to-all(bf16[4,192,896]{2,1,0:T(8,128)(2,1)S(1)} %shard_map.98), channel_id=1, replica_groups=mesh['node'=32,'x'=4,'y'=8] {'x'}, dimensions={0} | all-to-all | bytes 2752512 | tf_op jit(solution)/shard_map/all_to_all | solution.py:183
  179.9 0.0 copy-start.8
  179.9 0.2 shard_map.99
  180.1 15.9 %all_to_all.23.rows_ref = bf16[8,24,896]{2,1,0:T(8,128)(2,1)S(1)} all-to-all(bf16[8,24,896]{2,1,0:T(8,128)(2,1)S(1)} %bitcast.4), channel_id=1, replica_groups=mesh['node'=32,'x'=4,'y'=8] {'y'}, dimensions={0} | all-to-all | bytes 688128 | tf_op jit(solution)/shard_map/all_to_all | solution.py:185
  196.0 0.0 copy-done.8
  196.0 1.3 shard_map.100
Async XLA Ops:
  7.2 62.2 %all-gather.5.cloned.1.call-start = ((), (), s32[]{:S(2)}) async-start(), calls=%async_computation.4 | async-start | bytes 1720320 | tf_op jit(solution)/shard_map/all_gather | solution.py:169
  7.2 1.5 copy-start.1
  8.7 0.9 copy-start.4
  9.7 0.7 copy-start.7
  10.3 59.1 %copy-start = (bf16[2,896,512]{2,1,0:T(8,128)(2,1)S(1)}, bf16[2,896,512]{2,1,0:T(8,128)(2,1)}, u32[]{:S(2)}) copy-start(bf16[2,896,512]{2,1,0:T(8,128)(2,1)} %wg_ref.3) | copy-start | bytes 5505028
  10.3 59.1 %copy-start.6 = (bf16[192,192]{1,0:T(8,128)(2,1)S(1)}, bf16[192,192]{1,0:T(8,128)(2,1)}, u32[]{:S(2)}) copy-start(bf16[192,192]{1,0:T(8,128)(2,1)} %constant.4.clone.perm_ref) | copy-start | bytes 221188
  31.6 124.3 %all-gather.7.cloned.1.call-start = ((), (), s32[]{:S(2)}) async-start(), calls=%async_computation.5 | async-start | bytes 1327104 | tf_op jit(solution)/shard_map/all_gather | solution.py:177
  69.4 1.3 copy-start.2
  74.8 81.1 %copy-start.5 = (bf16[192,192]{1,0:T(8,128)(2,1)S(1)}, bf16[192,192]{1,0:T(8,128)(2,1)}, u32[]{:S(2)}) copy-start(bf16[192,192]{1,0:T(8,128)(2,1)} %constant.5.clone.back_ref) | copy-start | bytes 221188
  155.9 1.3 copy-start.3
  179.9 16.1 %copy-start.8 = (s32[128,8]{0,1:T(8,128)S(1)}, s32[128,8]{0,1:T(8,128)}, u32[]{:S(2)}) copy-start(s32[128,8]{0,1:T(8,128)} %param.10) | copy-start | bytes 12292
Sparse Core Ops, SparseCore 0:
  31.8 37.5 all-gather.4
  113.3 42.5 all-gather.6

commit v2 on v1

--- a/solution.py
+++ b/solution.py
@@ -48,14 +48,31 @@
     return jnp.where(hit, 1.0, 0.0)
 
 
-def pack_kernel(ids_ref, tok_ref, cot_ref, out_ref):
+def pack_kernel(ids_any, tok_any, cot_any, out_ref, ids_ref, tok_ref, cot_ref, sems):
+    width = out_ref.shape[2]
+    small = [
+        pltpu.make_async_copy(ids_any, ids_ref, sems.at[YS]),
+        pltpu.make_async_copy(cot_any, cot_ref, sems.at[YS + 1]),
+    ]
+    count = tok_ref.shape[0] // YS
+    large = [
+        pltpu.make_async_copy(
+            tok_any.at[pl.ds(s * count, count)], tok_ref.at[pl.ds(s * count, count)], sems.at[s]
+        )
+        for s in range(YS)
+    ]
+    for copy in small + large:
+        copy.start()
+    for copy in small:
+        copy.wait()
     onehot = slot_onehot(ids_ref[...], ROWS).astype(BF16)
     lift = (
         lax.broadcasted_iota(jnp.int32, (ROWS, SLOTS), 0)
         == lax.broadcasted_iota(jnp.int32, (ROWS, SLOTS), 1) + SLOTS
     )
     lift = jnp.where(lift, 1.0, 0.0).astype(BF16)
-    width = out_ref.shape[2]
+    for copy in large:
+        copy.wait()
     for s in range(YS):
         cols = slice(s * width, (s + 1) * width)
         out_ref[s] = (
@@ -63,7 +80,18 @@
         ).astype(BF16)
 
 
-def first_kernel(perm_ref, rows_ref, wg_ref, wu_ref, wd_ref, out_ref, lhs_ref):
+def copies_kernel(rows_ref, out_ref):
+    for xs in range(XS):
+        out_ref[xs] = rows_ref[...]
+
+
+def at(y, step):
+    return lax.rem(y + (step + YS), YS)
+
+
+def first_kernel(
+    perm_ref, rows_ref, wg_ref, wu_ref, wd_ref, up_ref, down_ref, keep_ref, lhs_ref, all_ref
+):
     block = YS * CAP
     for xs in range(XS):
         moved = dot_nn(perm_ref[...], rows_ref[xs]).astype(BF16)
@@ -75,20 +103,46 @@
         parts = (dot_nn(x, wg_ref[q]), dot_nn(x, wu_ref[q]), dot_nt(cot, wd_ref[q]))
         for j, part in enumerate(parts):
             hidden = part.shape[1]
-            out_ref[q * XS : (q + 1) * XS, :, j * hidden : (j + 1) * hidden] = part.astype(
-                BF16
-            ).reshape(XS, block, hidden)
-
-
-def act_kernel(sum_ref, out_ref):
+            all_ref[q * XS : (q + 1) * XS, :, j * hidden : (j + 1) * hidden] = part.reshape(
+                XS, block, hidden
+            )
+    y = lax.axis_index("y")
+    half = up_ref.shape[2]
+    for ref, sign in ((up_ref, 1), (down_ref, -1)):
+        for i, step in enumerate((sign, -2 * sign)):
+            for h in range(2):
+                ref[2 * i + h] = all_ref[at(y, step), :, h * half : (h + 1) * half].astype(BF16)
+    up_ref[4] = all_ref[at(y, 4), :, :half].astype(BF16)
+    down_ref[4] = all_ref[at(y, 4), :, half:].astype(BF16)
+    for i, step in enumerate((0, 3, -3)):
+        keep_ref[i] = all_ref[at(y, step)]
+
+
+def middle_kernel(keep_ref, below_ref, above_ref, own_ref, up_ref, down_ref):
+    half = below_ref.shape[2]
+    for h in range(2):
+        cols = slice(h * half, (h + 1) * half)
+        below = [below_ref[i].astype(F32) for i in (h, 2 + h)]
+        above = [above_ref[i].astype(F32) for i in (h, 2 + h)]
+        own_ref[:, cols] = keep_ref[0, :, cols] + below[0] + above[0]
+        up = keep_ref[1, :, cols] + above[1]
+        down = keep_ref[2, :, cols] + below[1]
+        if h == 0:
+            up = up + below_ref[4].astype(F32)
+        else:
+            down = down + above_ref[4].astype(F32)
+        up_ref[:, cols] = up.astype(BF16)
+        down_ref[:, cols] = down.astype(BF16)
+
+
+def act_kernel(own_ref, below_ref, above_ref, out_ref):
     hidden = out_ref.shape[1] // 3
 
     def total(j):
         cols = slice(j * hidden, (j + 1) * hidden)
-        value = sum_ref[0, :, cols].astype(F32)
-        for s in range(1, YS):
-            value = value + sum_ref[s, :, cols].astype(F32)
-        return value
+        return (
+            own_ref[:, cols] + below_ref[:, cols].astype(F32) + above_ref[:, cols].astype(F32)
+        )
 
     gate, up, grad = total(0), total(1), total(2)
     logistic = jax.nn.sigmoid(gate)
@@ -99,9 +153,48 @@
     out_ref[:, 2 * hidden :] = (grad * activation).astype(BF16)
 
 
-def second_kernel(back_ref, act_ref, wg_ref, wu_ref, wd_ref, out_ref, res_ref):
+def spread_kernel(own_ref, below_ref, above_ref, up_ref, down_ref):
+    half = up_ref.shape[2]
+    for h in range(2):
+        cols = slice(h * half, (h + 1) * half)
+        own, below, above = own_ref[:, cols], below_ref[:, cols], above_ref[:, cols]
+        up_ref[h], up_ref[2 + h] = own, above
+        down_ref[h], down_ref[2 + h] = own, below
+        if h == 0:
+            up_ref[4] = below
+        else:
+            down_ref[4] = above
+
+
+def second_kernel(
+    back_ref,
+    own_ref,
+    far_below_ref,
+    far_above_ref,
+    below_ref,
+    above_ref,
+    wg_ref,
+    wu_ref,
+    wd_ref,
+    out_ref,
+    res_ref,
+    act_ref,
+):
     block = YS * CAP
     hidden = act_ref.shape[2] // 3
+    half = below_ref.shape[2]
+    y = lax.axis_index("y")
+    act_ref[y] = own_ref[...]
+    act_ref[at(y, -3)] = far_below_ref[...]
+    act_ref[at(y, 3)] = far_above_ref[...]
+    for h in range(2):
+        cols = slice(h * half, (h + 1) * half)
+        act_ref[at(y, -1), :, cols] = below_ref[h]
+        act_ref[at(y, 2), :, cols] = below_ref[2 + h]
+        act_ref[at(y, 1), :, cols] = above_ref[h]
+        act_ref[at(y, -2), :, cols] = above_ref[2 + h]
+    act_ref[at(y, 4), :, :half] = below_ref[4]
+    act_ref[at(y, 4), :, half:] = above_ref[4]
     for q in range(2):
         mine = act_ref[q * XS : (q + 1) * XS].reshape(XS * block, 3 * hidden)
         out = dot_nn(mine[:, :hidden], wd_ref[q])
@@ -137,7 +230,7 @@
         grad_ref[:, cols] = dot_nn(pick_grad, rows_ref[s]).astype(BF16)
 
 
-def call(kernel, outs, scratch=(), vmem=48):
+def call(kernel, outs, scratch=(), vmem=12, space=pltpu.VMEM):
     spec = pl.BlockSpec(memory_space=pltpu.VMEM)
     single = not isinstance(outs, (tuple, list))
 
@@ -145,13 +238,17 @@
         return pl.pallas_call(
             kernel,
             out_shape=outs,
-            in_specs=[spec] * len(args),
+            in_specs=[pl.BlockSpec(memory_space=space)] * len(args),
             out_specs=spec if single else tuple(spec for _ in outs),
             scratch_shapes=list(scratch),
             compiler_params=pltpu.CompilerParams(vmem_limit_bytes=vmem * 1024 * 1024),
         )(*args)
 
     return run
+
+
+def shift(value, step):
+    return lax.ppermute(value, "y", [(i, (i + step) % YS) for i in range(YS)])
 
 
 def on_device(tokens, route_cot, expert_ids, w_gate, w_up, w_down):
@@ -164,22 +261,55 @@
     back = jnp.asarray(regroup().T, BF16)
     shape = jax.ShapeDtypeStruct
 
-    packed = call(pack_kernel, shape((YS, ROWS, part), BF16))(ids_t, tokens, route_cot)
+    packed = call(
+        pack_kernel,
+        shape((YS, ROWS, part), BF16),
+        [
+            pltpu.VMEM(ids_t.shape, jnp.int32),
+            pltpu.VMEM(tokens.shape, BF16),
+            pltpu.VMEM(route_cot.shape, BF16),
+            pltpu.SemaphoreType.DMA((YS + 2,)),
+        ],
+        vmem=60,
+        space=pltpu.HBM,
+    )(ids_t, tokens, route_cot)
     sliced = lax.all_to_all(packed, "y", split_axis=0, concat_axis=0, tiled=True)
-    rows = lax.all_gather(sliced, "x", axis=0, tiled=False).reshape(XS, YS * ROWS, part)
-    partials = call(
+    rows = lax.all_to_all(
+        call(copies_kernel, shape((XS, YS * ROWS, part), BF16))(sliced.reshape(YS * ROWS, part)),
+        "x",
+        split_axis=0,
+        concat_axis=0,
+        tiled=True,
+    )
+    halves = shape((5, block, 3 * hidden // 2), BF16)
+    chunk = shape((block, 3 * hidden), BF16)
+    up, down, keep = call(
         first_kernel,
-        shape((2 * XS, block, 3 * hidden), BF16),
-        [pltpu.VMEM((4, XS * block, part), BF16)],
+        (halves, halves, shape((3, block, 3 * hidden), F32)),
+        [
+            pltpu.VMEM((4, XS * block, part), BF16),
+            pltpu.VMEM((2 * XS, block, 3 * hidden), F32),
+        ],
+        24,
     )(perm, rows, w_gate, w_up, w_down)
-    shares = lax.all_to_all(partials, "y", split_axis=0, concat_axis=0, tiled=True)
-    acts = call(act_kernel, shape((block, 3 * hidden), BF16))(shares)
-    gathered = lax.all_gather(acts, "y", axis=0, tiled=False)
+    below, above = shift(up, 1), shift(down, -1)
+    own, up, down = call(middle_kernel, (shape(chunk.shape, F32), chunk, chunk))(
+        keep, below, above
+    )
+    below, above = shift(up, 3), shift(down, -3)
+    acts = call(act_kernel, chunk)(own, below, above)
+    far_below, far_above = shift(acts, 3), shift(acts, -3)
+    up, down = call(spread_kernel, (halves, halves))(acts, far_below, far_above)
+    below, above = shift(up, 1), shift(down, -1)
     results = call(
         second_kernel,
         shape((XS, YS * ROWS, part), BF16),
-        [pltpu.VMEM((XS, YS * ROWS, part), BF16)],
-    )(back, gathered, w_gate, w_up, w_down)
+        [
+            pltpu.VMEM((XS, YS * ROWS, part), BF16),
+            pltpu.VMEM((2 * XS, block, 3 * hidden), BF16),
+        ],
+        24,
+    )(back, acts, far_below, far_above, below, above, w_gate, w_up, w_down)
     blocks = lax.all_to_all(results, "x", split_axis=0, concat_axis=0, tiled=True)
     total = call(sum_kernel, shape((YS * ROWS, part), BF16))(blocks)
     home = lax.all_to_all(

time: 205 us -> 147 us (0.72)
  the two profiles are of different devices: /device:TPU:64 before, /device:TPU:960 now
where the time goes in v2:
time: 147 us; the launch traced here: 145 us
  blocking collectives  74.8 us (51%)
  starting transfers between devices  30.7 us (21%)
  waiting for transfers between devices  29.3 us (20%)
  Pallas kernels  9.26 us (6%)
    ppermute x8, starting transfers between devices, shift(): return lax.ppermute(value, 'y', [(i, (i + step) % YS) for i in range(YS)])  30.7 us
    ppermute x8, waiting for transfers between devices, shift(): return lax.ppermute(value, 'y', [(i, (i + step) % YS) for i in range(YS)])  29.3 us
    all_to_all x1, blocking collectives, on_device(): lax.all_to_all(call(copies_kernel, shape((XS, YS * ROWS, part), BF16))(sl...  21.4 us
    all_to_all x1, blocking collectives, on_device(): lax.all_to_all(packed, 'y', split_axis=0, concat_axis=0, tiled=True)  20.7 us
    all_to_all x1, blocking collectives, on_device(): lax.all_to_all(total.reshape(YS, ROWS, part), 'y', split_axis=0, concat_a...  17.5 us
    all_to_all x1, blocking collectives, on_device(): lax.all_to_all(results, 'x', split_axis=0, concat_axis=0, tiled=True)  15.1 us
    pallas_call x9, Pallas kernels, run(): pl.pallas_call(kernel, out_shape=outs, in_specs=[pl.BlockSpec(memory_spac...  9.26 us
  transfers between devices with their start and end apart: 8, of which 8 were waited for; matrix products, arithmetic and copies ran while one was open for 0% of the time, Pallas kernels for 0%

profile of v2, /device:TPU:960, one launch (start us, length us, event | category | flops | bytes accessed | tf_op | source)
XLA Modules:
  0.0 144.8 jit_solution(3704614094410069808)
XLA Ops:
  0.6 0.0 copy-start.2
  0.6 3.1 %shard_map.95 = bf16[8,24,896]{2,1,0:T(8,128)(2,1)} custom-call(s32[8,128]{1,0:T(8,128)} %bitcast.5, bf16[128,7168]{1,0:T(8,128)(2,1)} %tok_any.1, bf16[12,7168]{1,0:T(8,128)(2,1)} %cot_any.1), custom_call_target="tpu_custom_call" | custom-call | tf_op jit(solution)/shard_map/pallas_call | solution.py:238
  3.8 20.7 %all_to_all.20 = bf16[8,24,896]{2,1,0:T(8,128)(2,1)S(1)} all-to-all(bf16[8,24,896]{2,1,0:T(8,128)(2,1)} %shard_map.95), channel_id=1, replica_groups=mesh['node'=32,'x'=4,'y'=8] {'y'}, dimensions={0} | all-to-all | bytes 688128 | tf_op jit(solution)/shard_map/all_to_all | solution.py:276
  24.5 0.0 copy-start
  24.5 0.0 copy-start.1
  24.5 0.0 copy-start.4
  24.5 0.1 shard_map.96
  24.6 21.4 %all_to_all.21.rows_ref = bf16[4,192,896]{2,1,0:T(8,128)(2,1)S(1)} all-to-all(bf16[4,192,896]{2,1,0:T(8,128)(2,1)S(1)} %shard_map.96), channel_id=1, replica_groups=mesh['node'=32,'x'=4,'y'=8] {'x'}, dimensions={0} | all-to-all | bytes 2752512 | tf_op jit(solution)/shard_map/all_to_all | solution.py:277
  46.0 0.0 copy-done.2
  46.0 0.0 copy-done
  46.0 0.0 copy-done.1
  46.0 0.0 copy-done.4
  46.1 2.1 %shard_map.97 = (bf16[5,48,768]{2,1,0:T(8,128)(2,1)S(1)}, bf16[5,48,768]{2,1,0:T(8,128)(2,1)S(1)}, f32[3,48,1536]{2,1,0:T(8,128)S(1)}) custom-call(bf16[192,192]{1,0:T(8,128)(2,1)S(1)} %copy-done.4, bf16[4,192,896]{2,1,0:T(8,128)(2,1)S(1)} %all_to_all.21.rows_ref, bf16[2,896,512]{2,1,0:T(8,128)(2,1)S(1)} %copy-done, bf16[2,896,512]{2,1,0:T(8,128)(2,1)S(1)} %copy-done.1, ...), custom_call_target="tpu_custom_call" | custom-call | tf_op jit(solution)/shard_map/pallas_call | solution.py:238
  48.2 0.0 copy-start.3
  48.2 2.1 %collective-permute-start = (bf16[5,48,768]{2,1,0:T(8,128)(2,1)S(1)}, bf16[5,48,768]{2,1,0:T(8,128)(2,1)S(1)}, u32[]{:S(2)}, u32[]{:S(2)}) collective-permute-start(bf16[5,48,768]{2,1,0:T(8,128)(2,1)S(1)} %get-tuple-element.11), channel_id=1, source_target_pairs={{0,1},{1,2},{2,3},{3,4},{4,5},{5,6},{6,7},{7,0},{8,9},{9,10},{10,1... | collective-permute-start | bytes 1105928 | tf_op jit(solution)/shard_map/ppermute | solution.py:251
  50.3 5.1 %collective-permute-start.1 = (bf16[5,48,768]{2,1,0:T(8,128)(2,1)S(1)}, bf16[5,48,768]{2,1,0:T(8,128)(2,1)S(1)}, u32[]{:S(2)}, u32[]{:S(2)}) collective-permute-start(bf16[5,48,768]{2,1,0:T(8,128)(2,1)S(1)} %get-tuple-element.12), channel_id=1, source_target_pairs={{0,7},{1,0},{2,1},{3,2},{4,3},{5,4},{6,5},{7,6},{8,15},{9,8},{10,9... | collective-permute-start | bytes 1105928 | tf_op jit(solution)/shard_map/ppermute | solution.py:251
  55.4 3.5 %collective-permute-done.below_ref = bf16[5,48,768]{2,1,0:T(8,128)(2,1)S(1)} collective-permute-done((bf16[5,48,768]{2,1,0:T(8,128)(2,1)S(1)}, bf16[5,48,768]{2,1,0:T(8,128)(2,1)S(1)}, u32[]{:S(2)}, u32[]{:S(2)}) %collective-permute-start) | collective-permute-done | bytes 368672 | tf_op jit(solution)/shard_map/ppermute | solution.py:251
  58.9 1.5 %collective-permute-done.1.above_ref = bf16[5,48,768]{2,1,0:T(8,128)(2,1)S(1)} collective-permute-done((bf16[5,48,768]{2,1,0:T(8,128)(2,1)S(1)}, bf16[5,48,768]{2,1,0:T(8,128)(2,1)S(1)}, u32[]{:S(2)}, u32[]{:S(2)}) %collective-permute-start.1) | collective-permute-done | bytes 368672 | tf_op jit(solution)/shard_map/ppermute | solution.py:251
  60.4 0.1 shard_map.98
  60.5 4.7 %collective-permute-start.2 = (bf16[48,1536]{1,0:T(8,128)(2,1)S(1)}, bf16[48,1536]{1,0:T(8,128)(2,1)S(1)}, u32[]{:S(2)}, u32[]{:S(2)}) collective-permute-start(bf16[48,1536]{1,0:T(8,128)(2,1)S(1)} %get-tuple-element.14), channel_id=1, source_target_pairs={{0,3},{1,4},{2,5},{3,6},{4,7},{5,0},{6,1},{7,2},{8,11},{9,12},{10,... | collective-permute-start | bytes 442376 | tf_op jit(solution)/shard_map/ppermute | solution.py:251
  65.2 4.2 %collective-permute-start.3 = (bf16[48,1536]{1,0:T(8,128)(2,1)S(1)}, bf16[48,1536]{1,0:T(8,128)(2,1)S(1)}, u32[]{:S(2)}, u32[]{:S(2)}) collective-permute-start(bf16[48,1536]{1,0:T(8,128)(2,1)S(1)} %get-tuple-element.15), channel_id=1, source_target_pairs={{0,5},{1,6},{2,7},{3,0},{4,1},{5,2},{6,3},{7,4},{8,13},{9,14},{10,... | collective-permute-start | bytes 442376 | tf_op jit(solution)/shard_map/ppermute | solution.py:251
  69.4 1.2 collective-permute-done.2.below_ref
  70.6 5.9 %collective-permute-done.3.above_ref = bf16[48,1536]{1,0:T(8,128)(2,1)S(1)} collective-permute-done((bf16[48,1536]{1,0:T(8,128)(2,1)S(1)}, bf16[48,1536]{1,0:T(8,128)(2,1)S(1)}, u32[]{:S(2)}, u32[]{:S(2)}) %collective-permute-start.3) | collective-permute-done | bytes 147488 | tf_op jit(solution)/shard_map/ppermute | solution.py:251
  76.5 0.1 shard_map.99.own_ref
  76.6 5.5 %collective-permute-start.5 = (bf16[48,1536]{1,0:T(8,128)(2,1)S(1)}, bf16[48,1536]{1,0:T(8,128)(2,1)S(1)}, u32[]{:S(2)}, u32[]{:S(2)}) collective-permute-start(bf16[48,1536]{1,0:T(8,128)(2,1)S(1)} %shard_map.99.own_ref), channel_id=1, source_target_pairs={{0,5},{1,6},{2,7},{3,0},{4,1},{5,2},{6,3},{7,4},{8,13},{9,14},{10,... | collective-permute-start | bytes 442376 | tf_op jit(solution)/shard_map/ppermute | solution.py:251
  82.1 2.1 %collective-permute-start.4 = (bf16[48,1536]{1,0:T(8,128)(2,1)S(1)}, bf16[48,1536]{1,0:T(8,128)(2,1)S(1)}, u32[]{:S(2)}, u32[]{:S(2)}) collective-permute-start(bf16[48,1536]{1,0:T(8,128)(2,1)S(1)} %shard_map.99.own_ref), channel_id=1, source_target_pairs={{0,3},{1,4},{2,5},{3,6},{4,7},{5,0},{6,1},{7,2},{8,11},{9,12},{10,... | collective-permute-start | bytes 442376 | tf_op jit(solution)/shard_map/ppermute | solution.py:251
  84.2 1.8 %collective-permute-done.5.above_ref.far_above_ref = bf16[48,1536]{1,0:T(8,128)(2,1)S(1)} collective-permute-done((bf16[48,1536]{1,0:T(8,128)(2,1)S(1)}, bf16[48,1536]{1,0:T(8,128)(2,1)S(1)}, u32[]{:S(2)}, u32[]{:S(2)}) %collective-permute-start.5) | collective-permute-done | bytes 147488 | tf_op jit(solution)/shard_map/ppermute | solution.py:251
  86.0 10.3 %collective-permute-done.4.below_ref.far_below_ref = bf16[48,1536]{1,0:T(8,128)(2,1)S(1)} collective-permute-done((bf16[48,1536]{1,0:T(8,128)(2,1)S(1)}, bf16[48,1536]{1,0:T(8,128)(2,1)S(1)}, u32[]{:S(2)}, u32[]{:S(2)}) %collective-permute-start.4) | collective-permute-done | bytes 147488 | tf_op jit(solution)/shard_map/ppermute | solution.py:251
  96.4 1.9 %collective-permute-start.6 = (bf16[5,48,768]{2,1,0:T(8,128)(2,1)S(1)}, bf16[5,48,768]{2,1,0:T(8,128)(2,1)S(1)}, u32[]{:S(2)}, u32[]{:S(2)}) collective-permute-start(bf16[5,48,768]{2,1,0:T(8,128)(2,1)S(1)} %get-tuple-element.16), channel_id=1, source_target_pairs={{0,1},{1,2},{2,3},{3,4},{4,5},{5,6},{6,7},{7,0},{8,9},{9,10},{10,1... | collective-permute-start | bytes 1105928 | tf_op jit(solution)/shard_map/ppermute | solution.py:251
  98.4 5.1 %collective-permute-start.7 = (bf16[5,48,768]{2,1,0:T(8,128)(2,1)S(1)}, bf16[5,48,768]{2,1,0:T(8,128)(2,1)S(1)}, u32[]{:S(2)}, u32[]{:S(2)}) collective-permute-start(bf16[5,48,768]{2,1,0:T(8,128)(2,1)S(1)} %get-tuple-element.17), channel_id=1, source_target_pairs={{0,7},{1,0},{2,1},{3,2},{4,3},{5,4},{6,5},{7,6},{8,15},{9,8},{10,9... | collective-permute-start | bytes 1105928 | tf_op jit(solution)/shard_map/ppermute | solution.py:251
  103.5 3.5 %collective-permute-done.6.below_ref = bf16[5,48,768]{2,1,0:T(8,128)(2,1)S(1)} collective-permute-done((bf16[5,48,768]{2,1,0:T(8,128)(2,1)S(1)}, bf16[5,48,768]{2,1,0:T(8,128)(2,1)S(1)}, u32[]{:S(2)}, u32[]{:S(2)}) %collective-permute-start.6) | collective-permute-done | bytes 368672 | tf_op jit(solution)/shard_map/ppermute | solution.py:251
  107.1 1.5 %collective-permute-done.7.above_ref = bf16[5,48,768]{2,1,0:T(8,128)(2,1)S(1)} collective-permute-done((bf16[5,48,768]{2,1,0:T(8,128)(2,1)S(1)}, bf16[5,48,768]{2,1,0:T(8,128)(2,1)S(1)}, u32[]{:S(2)}, u32[]{:S(2)}) %collective-permute-start.7) | collective-permute-done | bytes 368672 | tf_op jit(solution)/shard_map/ppermute | solution.py:251
  108.5 0.0 copy-done.3
  108.5 2.2 %shard_map.101 = bf16[4,192,896]{2,1,0:T(8,128)(2,1)S(1)} custom-call(bf16[192,192]{1,0:T(8,128)(2,1)S(1)} %copy-done.3, bf16[48,1536]{1,0:T(8,128)(2,1)S(1)} %shard_map.99.own_ref, bf16[48,1536]{1,0:T(8,128)(2,1)S(1)} %collective-permute-done.4.below_ref.far_below_ref, bf16[48,1536]{1,0:T(8,128)(2,1)S(1)} %collective-permute-done.5.above_ref.far_above_ref, ...), custom_call_target="tpu_custom_call" | custom-call | tf_op jit(solution)/shard_map/pallas_call | solution.py:238
  110.8 15.1 %all_to_all.22.parts_ref = bf16[4,192,896]{2,1,0:T(8,128)(2,1)S(1)} all-to-all(bf16[4,192,896]{2,1,0:T(8,128)(2,1)S(1)} %shard_map.101), channel_id=1, replica_groups=mesh['node'=32,'x'=4,'y'=8] {'x'}, dimensions={0} | all-to-all | bytes 2752512 | tf_op jit(solution)/shard_map/all_to_all | solution.py:313
  125.8 0.0 copy-start.5
  125.8 0.2 shard_map.102
  126.0 17.5 %all_to_all.23.rows_ref = bf16[8,24,896]{2,1,0:T(8,128)(2,1)S(1)} all-to-all(bf16[8,24,896]{2,1,0:T(8,128)(2,1)S(1)} %bitcast.4), channel_id=1, replica_groups=mesh['node'=32,'x'=4,'y'=8] {'y'}, dimensions={0} | all-to-all | bytes 688128 | tf_op jit(solution)/shard_map/all_to_all | solution.py:315
  143.6 0.0 copy-done.5
  143.6 1.3 shard_map.103
  (1 shorter events, 0.0 us)
Async XLA Ops:
  0.6 45.4 %copy-start.2 = (bf16[2,512,896]{2,1,0:T(8,128)(2,1)S(1)}, bf16[2,512,896]{2,1,0:T(8,128)(2,1)}, u32[]{:S(2)}) copy-start(bf16[2,512,896]{2,1,0:T(8,128)(2,1)} %wd_ref.3) | copy-start | bytes 5505028
  24.5 21.5 %copy-start = (bf16[2,896,512]{2,1,0:T(8,128)(2,1)S(1)}, bf16[2,896,512]{2,1,0:T(8,128)(2,1)}, u32[]{:S(2)}) copy-start(bf16[2,896,512]{2,1,0:T(8,128)(2,1)} %wg_ref.3) | copy-start | bytes 5505028
  24.5 21.5 %copy-start.1 = (bf16[2,896,512]{2,1,0:T(8,128)(2,1)S(1)}, bf16[2,896,512]{2,1,0:T(8,128)(2,1)}, u32[]{:S(2)}) copy-start(bf16[2,896,512]{2,1,0:T(8,128)(2,1)} %wu_ref.3) | copy-start | bytes 5505028
  24.5 21.5 %copy-start.4 = (bf16[192,192]{1,0:T(8,128)(2,1)S(1)}, bf16[192,192]{1,0:T(8,128)(2,1)}, u32[]{:S(2)}) copy-start(bf16[192,192]{1,0:T(8,128)(2,1)} %constant.4.clone.perm_ref) | copy-start | bytes 221188
  48.2 60.3 %copy-start.3 = (bf16[192,192]{1,0:T(8,128)(2,1)S(1)}, bf16[192,192]{1,0:T(8,128)(2,1)}, u32[]{:S(2)}) copy-start(bf16[192,192]{1,0:T(8,128)(2,1)} %constant.5.clone.back_ref) | copy-start | bytes 221188
  48.2 10.7 %collective-permute-start = (bf16[5,48,768]{2,1,0:T(8,128)(2,1)S(1)}, bf16[5,48,768]{2,1,0:T(8,128)(2,1)S(1)}, u32[]{:S(2)}, u32[]{:S(2)}) collective-permute-start(bf16[5,48,768]{2,1,0:T(8,128)(2,1)S(1)} %get-tuple-element.11), channel_id=1, source_target_pairs={{0,1},{1,2},{2,3},{3,4},{4,5},{5,6},{6,7},{7,0},{8,9},{9,10},{10,1... | collective-permute-start | bytes 1105928 | tf_op jit(solution)/shard_map/ppermute | solution.py:251
  50.3 10.2 %collective-permute-start.1 = (bf16[5,48,768]{2,1,0:T(8,128)(2,1)S(1)}, bf16[5,48,768]{2,1,0:T(8,128)(2,1)S(1)}, u32[]{:S(2)}, u32[]{:S(2)}) collective-permute-start(bf16[5,48,768]{2,1,0:T(8,128)(2,1)S(1)} %get-tuple-element.12), channel_id=1, source_target_pairs={{0,7},{1,0},{2,1},{3,2},{4,3},{5,4},{6,5},{7,6},{8,15},{9,8},{10,9... | collective-permute-start | bytes 1105928 | tf_op jit(solution)/shard_map/ppermute | solution.py:251
  60.5 10.0 %collective-permute-start.2 = (bf16[48,1536]{1,0:T(8,128)(2,1)S(1)}, bf16[48,1536]{1,0:T(8,128)(2,1)S(1)}, u32[]{:S(2)}, u32[]{:S(2)}) collective-permute-start(bf16[48,1536]{1,0:T(8,128)(2,1)S(1)} %get-tuple-element.14), channel_id=1, source_target_pairs={{0,3},{1,4},{2,5},{3,6},{4,7},{5,0},{6,1},{7,2},{8,11},{9,12},{10,... | collective-permute-start | bytes 442376 | tf_op jit(solution)/shard_map/ppermute | solution.py:251
  65.2 11.2 %collective-permute-start.3 = (bf16[48,1536]{1,0:T(8,128)(2,1)S(1)}, bf16[48,1536]{1,0:T(8,128)(2,1)S(1)}, u32[]{:S(2)}, u32[]{:S(2)}) collective-permute-start(bf16[48,1536]{1,0:T(8,128)(2,1)S(1)} %get-tuple-element.15), channel_id=1, source_target_pairs={{0,5},{1,6},{2,7},{3,0},{4,1},{5,2},{6,3},{7,4},{8,13},{9,14},{10,... | collective-permute-start | bytes 442376 | tf_op jit(solution)/shard_map/ppermute | solution.py:251
  76.6 9.5 %collective-permute-start.5 = (bf16[48,1536]{1,0:T(8,128)(2,1)S(1)}, bf16[48,1536]{1,0:T(8,128)(2,1)S(1)}, u32[]{:S(2)}, u32[]{:S(2)}) collective-permute-start(bf16[48,1536]{1,0:T(8,128)(2,1)S(1)} %shard_map.99.own_ref), channel_id=1, source_target_pairs={{0,5},{1,6},{2,7},{3,0},{4,1},{5,2},{6,3},{7,4},{8,13},{9,14},{10,... | collective-permute-start | bytes 442376 | tf_op jit(solution)/shard_map/ppermute | solution.py:251
  82.1 14.3 %collective-permute-start.4 = (bf16[48,1536]{1,0:T(8,128)(2,1)S(1)}, bf16[48,1536]{1,0:T(8,128)(2,1)S(1)}, u32[]{:S(2)}, u32[]{:S(2)}) collective-permute-start(bf16[48,1536]{1,0:T(8,128)(2,1)S(1)} %shard_map.99.own_ref), channel_id=1, source_target_pairs={{0,3},{1,4},{2,5},{3,6},{4,7},{5,0},{6,1},{7,2},{8,11},{9,12},{10,... | collective-permute-start | bytes 442376 | tf_op jit(solution)/shard_map/ppermute | solution.py:251
  96.4 10.6 %collective-permute-start.6 = (bf16[5,48,768]{2,1,0:T(8,128)(2,1)S(1)}, bf16[5,48,768]{2,1,0:T(8,128)(2,1)S(1)}, u32[]{:S(2)}, u32[]{:S(2)}) collective-permute-start(bf16[5,48,768]{2,1,0:T(8,128)(2,1)S(1)} %get-tuple-element.16), channel_id=1, source_target_pairs={{0,1},{1,2},{2,3},{3,4},{4,5},{5,6},{6,7},{7,0},{8,9},{9,10},{10,1... | collective-permute-start | bytes 1105928 | tf_op jit(solution)/shard_map/ppermute | solution.py:251
  98.4 10.2 %collective-permute-start.7 = (bf16[5,48,768]{2,1,0:T(8,128)(2,1)S(1)}, bf16[5,48,768]{2,1,0:T(8,128)(2,1)S(1)}, u32[]{:S(2)}, u32[]{:S(2)}) collective-permute-start(bf16[5,48,768]{2,1,0:T(8,128)(2,1)S(1)} %get-tuple-element.17), channel_id=1, source_target_pairs={{0,7},{1,0},{2,1},{3,2},{4,3},{5,4},{6,5},{7,6},{8,15},{9,8},{10,9... | collective-permute-start | bytes 1105928 | tf_op jit(solution)/shard_map/ppermute | solution.py:251
  125.8 17.7 %copy-start.5 = (s32[128,8]{0,1:T(8,128)S(1)}, s32[128,8]{0,1:T(8,128)}, u32[]{:S(2)}) copy-start(s32[128,8]{0,1:T(8,128)} %param.10) | copy-start | bytes 12292

commit v3 on v1

--- a/solution.py
+++ b/solution.py
@@ -48,19 +48,41 @@
     return jnp.where(hit, 1.0, 0.0)
 
 
-def pack_kernel(ids_ref, tok_ref, cot_ref, out_ref):
+def pack_kernel(ids_any, tok_any, cot_any, out_ref, ids_ref, tok_ref, cot_ref, sems):
+    width = out_ref.shape[2]
+    small = [
+        pltpu.make_async_copy(ids_any, ids_ref, sems.at[YS]),
+        pltpu.make_async_copy(cot_any, cot_ref, sems.at[YS + 1]),
+    ]
+    count = tok_ref.shape[0] // YS
+    large = [
+        pltpu.make_async_copy(
+            tok_any.at[pl.ds(s * count, count)], tok_ref.at[pl.ds(s * count, count)], sems.at[s]
+        )
+        for s in range(YS)
+    ]
+    for copy in small + large:
+        copy.start()
+    for copy in small:
+        copy.wait()
     onehot = slot_onehot(ids_ref[...], ROWS).astype(BF16)
     lift = (
         lax.broadcasted_iota(jnp.int32, (ROWS, SLOTS), 0)
         == lax.broadcasted_iota(jnp.int32, (ROWS, SLOTS), 1) + SLOTS
     )
     lift = jnp.where(lift, 1.0, 0.0).astype(BF16)
-    width = out_ref.shape[2]
+    for copy in large:
+        copy.wait()
     for s in range(YS):
         cols = slice(s * width, (s + 1) * width)
         out_ref[s] = (
             dot_nn(onehot, tok_ref[:, cols]) + dot_nn(lift, cot_ref[:, cols])
         ).astype(BF16)
+
+
+def copies_kernel(rows_ref, out_ref):
+    for xs in range(XS):
+        out_ref[xs] = rows_ref[...]
 
 
 def first_kernel(perm_ref, rows_ref, wg_ref, wu_ref, wd_ref, out_ref, lhs_ref):
@@ -80,23 +102,25 @@
             ).reshape(XS, block, hidden)
 
 
-def act_kernel(sum_ref, out_ref):
-    hidden = out_ref.shape[1] // 3
+def act_kernel(parts_ref, out_ref):
+    hidden = out_ref.shape[2] // 3
 
     def total(j):
         cols = slice(j * hidden, (j + 1) * hidden)
-        value = sum_ref[0, :, cols].astype(F32)
+        value = parts_ref[0, :, cols].astype(F32)
         for s in range(1, YS):
-            value = value + sum_ref[s, :, cols].astype(F32)
+            value = value + parts_ref[s, :, cols].astype(F32)
         return value
 
     gate, up, grad = total(0), total(1), total(2)
     logistic = jax.nn.sigmoid(gate)
     activation = gate * logistic
     slope = logistic * (1.0 + gate * (1.0 - logistic))
-    out_ref[:, :hidden] = (activation * up).astype(BF16)
-    out_ref[:, hidden : 2 * hidden] = (grad * up * slope).astype(BF16)
-    out_ref[:, 2 * hidden :] = (grad * activation).astype(BF16)
+    values = (activation * up, grad * up * slope, grad * activation)
+    for j, value in enumerate(values):
+        value = value.astype(BF16)
+        for s in range(YS):
+            out_ref[s, :, j * hidden : (j + 1) * hidden] = value
 
 
 def second_kernel(back_ref, act_ref, wg_ref, wu_ref, wd_ref, out_ref, res_ref):
@@ -137,7 +161,7 @@
         grad_ref[:, cols] = dot_nn(pick_grad, rows_ref[s]).astype(BF16)
 
 
-def call(kernel, outs, scratch=(), vmem=48):
+def call(kernel, outs, scratch=(), vmem=12, space=pltpu.VMEM):
     spec = pl.BlockSpec(memory_space=pltpu.VMEM)
     single = not isinstance(outs, (tuple, list))
 
@@ -145,13 +169,21 @@
         return pl.pallas_call(
             kernel,
             out_shape=outs,
-            in_specs=[spec] * len(args),
+            in_specs=[pl.BlockSpec(memory_space=space)] * len(args),
             out_specs=spec if single else tuple(spec for _ in outs),
             scratch_shapes=list(scratch),
             compiler_params=pltpu.CompilerParams(vmem_limit_bytes=vmem * 1024 * 1024),
         )(*args)
 
     return run
+
+
+def send_whole(packed):
+    return lax.all_to_all(packed, "y", split_axis=0, concat_axis=0, tiled=True)
+
+
+def send_in_pieces(packed):
+    return jnp.concatenate([send_whole(packed[:, :8]), send_whole(packed[:, 8:])], axis=1)
 
 
 def on_device(tokens, route_cot, expert_ids, w_gate, w_up, w_down):
@@ -164,22 +196,41 @@
     back = jnp.asarray(regroup().T, BF16)
     shape = jax.ShapeDtypeStruct
 
-    packed = call(pack_kernel, shape((YS, ROWS, part), BF16))(ids_t, tokens, route_cot)
-    sliced = lax.all_to_all(packed, "y", split_axis=0, concat_axis=0, tiled=True)
-    rows = lax.all_gather(sliced, "x", axis=0, tiled=False).reshape(XS, YS * ROWS, part)
-    partials = call(
-        first_kernel,
-        shape((2 * XS, block, 3 * hidden), BF16),
-        [pltpu.VMEM((4, XS * block, part), BF16)],
-    )(perm, rows, w_gate, w_up, w_down)
+    packed = call(
+        pack_kernel,
+        shape((YS, ROWS, part), BF16),
+        [
+            pltpu.VMEM(ids_t.shape, jnp.int32),
+            pltpu.VMEM(tokens.shape, BF16),
+            pltpu.VMEM(route_cot.shape, BF16),
+            pltpu.SemaphoreType.DMA((YS + 2,)),
+        ],
+        vmem=60,
+        space=pltpu.HBM,
+    )(ids_t, tokens, route_cot)
+    sliced = lax.cond(
+        lax.rem(lax.axis_index("node"), 2) == 0, send_in_pieces, send_whole, packed
+    )
+    rows = lax.all_to_all(
+        call(copies_kernel, shape((XS, YS * ROWS, part), BF16))(sliced.reshape(YS * ROWS, part)),
+        "x",
+        split_axis=0,
+        concat_axis=0,
+        tiled=True,
+    )
+    chunks = shape((2 * XS, block, 3 * hidden), BF16)
+    partials = call(first_kernel, chunks, [pltpu.VMEM((4, XS * block, part), BF16)], 24)(
+        perm, rows, w_gate, w_up, w_down
+    )
     shares = lax.all_to_all(partials, "y", split_axis=0, concat_axis=0, tiled=True)
-    acts = call(act_kernel, shape((block, 3 * hidden), BF16))(shares)
-    gathered = lax.all_gather(acts, "y", axis=0, tiled=False)
+    acts = call(act_kernel, chunks)(shares)
+    acts = lax.all_to_all(acts, "y", split_axis=0, concat_axis=0, tiled=True)
     results = call(
         second_kernel,
         shape((XS, YS * ROWS, part), BF16),
         [pltpu.VMEM((XS, YS * ROWS, part), BF16)],
-    )(back, gathered, w_gate, w_up, w_down)
+        24,
+    )(back, acts, w_gate, w_up, w_down)
     blocks = lax.all_to_all(results, "x", split_axis=0, concat_axis=0, tiled=True)
     total = call(sum_kernel, shape((YS * ROWS, part), BF16))(blocks)
     home = lax.all_to_all(

time: 205 us -> 147 us (0.72)
  the two profiles are of different devices: /device:TPU:64 before, /device:TPU:2 now
where the time goes in v3:
time: 147 us
  blocking collectives  120 us (82%)
  waiting for transfers between devices  10.4 us (7%)
  Pallas kernels  8.17 us (6%)
  starting transfers between devices  7.1 us (5%)
    all_to_all x1, blocking collectives, on_device(): lax.all_to_all(partials, 'y', split_axis=0, concat_axis=0, tiled=True)  33.6 us
    all_to_all x1, blocking collectives, on_device(): acts = lax.all_to_all(acts, 'y', split_axis=0, concat_axis=0, tiled=True)  23.2 us
    all_to_all x1, blocking collectives, on_device(): lax.all_to_all(call(copies_kernel, shape((XS, YS * ROWS, part), BF16))(sl...  21.7 us
    all_to_all x1, blocking collectives, on_device(): lax.all_to_all(results, 'x', split_axis=0, concat_axis=0, tiled=True)  15 us
    all_to_all x1, blocking collectives, on_device(): lax.all_to_all(total.reshape(YS, ROWS, part), 'y', split_axis=0, concat_a...  13.7 us
    all_to_all x1, blocking collectives, send_whole(): return lax.all_to_all(packed, 'y', split_axis=0, concat_axis=0, tiled=True)  12.5 us
    all_to_all x1, waiting for transfers between devices, send_whole(): return lax.all_to_all(packed, 'y', split_axis=0, concat_axis=0, tiled=True)  10.4 us
    pallas_call x7, Pallas kernels, run(): pl.pallas_call(kernel, out_shape=outs, in_specs=[pl.BlockSpec(memory_spac...  8.17 us
  transfers between devices with their start and end apart: 1, of which 1 were waited for; matrix products, arithmetic and copies ran while one was open for 0% of the time, Pallas kernels for 0%

profile of v3, /device:TPU:2, one launch (start us, length us, event | category | flops | bytes accessed | tf_op | source)
XLA Modules:
  0.0 147.0 jit_solution(4173472777681860648)
XLA Ops:
  0.6 2.3 %shard_map.95 = bf16[8,24,896]{2,1,0:T(8,128)(2,1)S(1)} custom-call(s32[8,128]{1,0:T(8,128)} %bitcast.4, bf16[128,7168]{1,0:T(8,128)(2,1)} %tok_any.1, bf16[12,7168]{1,0:T(8,128)(2,1)} %cot_any.1), custom_call_target="tpu_custom_call" | custom-call | tf_op jit(solution)/shard_map/pallas_call | solution.py:169
  2.9 0.0 copy-start.2
  2.9 30.7 %conditional.1 = (bf16[8,24,896]{2,1,0:T(8,128)(2,1)S(1)}) conditional(s32[]{:T(128)} %convert_element_type.3, bf16[8,24,896]{2,1,0:T(8,128)(2,1)S(1)} %shard_map.95, bf16[8,24,896]{2,1,0:T(8,128)(2,1)S(1)} %shard_map.95), branch_computations={%region_0.0_spmd, %region_1.0_spmd} | conditional | flops 688128 | bytes 2179112 | solution.py:211
  2.9 0.7 slice.4
  3.6 7.1 %all-to-all-start.1 = ((bf16[8,8,896]{2,1,0:T(8,128)(2,1)}), bf16[8,8,896]{2,1,0:T(8,128)(2,1)S(1)}, u32[]{:S(2)}, u32[]{:S(2)}) async-start(bf16[8,8,896]{2,1,0:T(8,128)(2,1)} %slice.4), calls=%async_computation.1 | async-start | bytes 229376 | tf_op jit(solution)/shard_map/cond/branch_1_fun/all_to_all | solution.py:182
  10.7 10.4 %all-to-all-done.1 = bf16[8,8,896]{2,1,0:T(8,128)(2,1)S(1)} async-done(((bf16[8,8,896]{2,1,0:T(8,128)(2,1)}), bf16[8,8,896]{2,1,0:T(8,128)(2,1)S(1)}, u32[]{:S(2)}, u32[]{:S(2)}) %all-to-all-start.1) | async-done | bytes 114720 | tf_op jit(solution)/shard_map/cond/branch_1_fun/all_to_all | solution.py:182
  21.1 12.5 %all_to_all.38 = bf16[8,16,896]{2,1,0:T(8,128)(2,1)S(1)} all-to-all(bf16[8,16,896]{2,1,0:T(8,128)(2,1)S(1)} %slice.5), channel_id=1, replica_groups=mesh['node'=32,'x'=4,'y'=8] {'y'}, dimensions={0} | all-to-all | bytes 458752 | tf_op jit(solution)/shard_map/cond/branch_1_fun/all_to_all | solution.py:182
  33.7 0.0 copy-start.1
  33.7 0.1 shard_map.96
  33.8 0.0 copy-start
  33.8 0.0 copy-start.4
  33.8 21.7 %all_to_all.39.rows_ref = bf16[4,192,896]{2,1,0:T(8,128)(2,1)S(1)} all-to-all(bf16[4,192,896]{2,1,0:T(8,128)(2,1)S(1)} %shard_map.96), channel_id=1, replica_groups=mesh['node'=32,'x'=4,'y'=8] {'x'}, dimensions={0} | all-to-all | bytes 2752512 | tf_op jit(solution)/shard_map/all_to_all | solution.py:214
  55.5 0.0 copy-done.2
  55.5 0.0 copy-done.1
  55.6 0.0 copy-done
  55.6 0.0 copy-done.4
  55.6 2.0 %shard_map.97 = bf16[8,48,1536]{2,1,0:T(8,128)(2,1)S(1)} custom-call(bf16[192,192]{1,0:T(8,128)(2,1)S(1)} %copy-done.4, bf16[4,192,896]{2,1,0:T(8,128)(2,1)S(1)} %all_to_all.39.rows_ref, bf16[2,896,512]{2,1,0:T(8,128)(2,1)S(1)} %copy-done, bf16[2,896,512]{2,1,0:T(8,128)(2,1)S(1)} %copy-done.1, bf16[2,512,896]{2,1,0:T(8,128)(2,1)S(1)} %copy-done.2), custom_call_target="tpu_custom_call" | custom-call | tf_op jit(solution)/shard_map/pallas_call | solution.py:169
  57.6 33.6 %all_to_all.40.parts_ref = bf16[8,48,1536]{2,1,0:T(8,128)(2,1)S(1)} all-to-all(bf16[8,48,1536]{2,1,0:T(8,128)(2,1)S(1)} %shard_map.97), channel_id=1, replica_groups=mesh['node'=32,'x'=4,'y'=8] {'y'}, dimensions={0} | all-to-all | bytes 2359296 | tf_op jit(solution)/shard_map/all_to_all | solution.py:225
  91.2 0.2 shard_map.98
  91.4 0.0 copy-start.3
  91.4 23.2 %all_to_all.41.act_ref = bf16[8,48,1536]{2,1,0:T(8,128)(2,1)S(1)} all-to-all(bf16[8,48,1536]{2,1,0:T(8,128)(2,1)S(1)} %shard_map.98), channel_id=1, replica_groups=mesh['node'=32,'x'=4,'y'=8] {'y'}, dimensions={0} | all-to-all | bytes 2359296 | tf_op jit(solution)/shard_map/all_to_all | solution.py:227
  114.6 0.0 copy-done.3
  114.6 2.2 %shard_map.99 = bf16[4,192,896]{2,1,0:T(8,128)(2,1)S(1)} custom-call(bf16[192,192]{1,0:T(8,128)(2,1)S(1)} %copy-done.3, bf16[8,48,1536]{2,1,0:T(8,128)(2,1)S(1)} %all_to_all.41.act_ref, bf16[2,896,512]{2,1,0:T(8,128)(2,1)S(1)} %copy-done, bf16[2,896,512]{2,1,0:T(8,128)(2,1)S(1)} %copy-done.1, bf16[2,512,896]{2,1,0:T(8,128)(2,1)S(1)} %copy-done.2), custom_call_target="tpu_custom_call" | custom-call | tf_op jit(solution)/shard_map/pallas_call | solution.py:169
  116.8 15.0 %all_to_all.42.parts_ref = bf16[4,192,896]{2,1,0:T(8,128)(2,1)S(1)} all-to-all(bf16[4,192,896]{2,1,0:T(8,128)(2,1)S(1)} %shard_map.99), channel_id=1, replica_groups=mesh['node'=32,'x'=4,'y'=8] {'x'}, dimensions={0} | all-to-all | bytes 2752512 | tf_op jit(solution)/shard_map/all_to_all | solution.py:234
  131.8 0.0 copy-start.5
  131.8 0.2 shard_map.100
  132.0 13.7 %all_to_all.43.rows_ref = bf16[8,24,896]{2,1,0:T(8,128)(2,1)S(1)} all-to-all(bf16[8,24,896]{2,1,0:T(8,128)(2,1)S(1)} %bitcast.3), channel_id=1, replica_groups=mesh['node'=32,'x'=4,'y'=8] {'y'}, dimensions={0} | all-to-all | bytes 688128 | tf_op jit(solution)/shard_map/all_to_all | solution.py:236
  145.7 0.0 copy-done.5
  145.7 1.3 shard_map.101
  (2 shorter events, 0.0 us)
Async XLA Ops:
  2.9 52.6 %copy-start.2 = (bf16[2,512,896]{2,1,0:T(8,128)(2,1)S(1)}, bf16[2,512,896]{2,1,0:T(8,128)(2,1)}, u32[]{:S(2)}) copy-start(bf16[2,512,896]{2,1,0:T(8,128)(2,1)} %wd_ref.3) | copy-start | bytes 5505028
  3.6 17.5 %all-to-all-start.1 = ((bf16[8,8,896]{2,1,0:T(8,128)(2,1)}), bf16[8,8,896]{2,1,0:T(8,128)(2,1)S(1)}, u32[]{:S(2)}, u32[]{:S(2)}) async-start(bf16[8,8,896]{2,1,0:T(8,128)(2,1)} %slice.4), calls=%async_computation.1 | async-start | bytes 229376 | tf_op jit(solution)/shard_map/cond/branch_1_fun/all_to_all | solution.py:182
  33.7 21.9 %copy-start.1 = (bf16[2,896,512]{2,1,0:T(8,128)(2,1)S(1)}, bf16[2,896,512]{2,1,0:T(8,128)(2,1)}, u32[]{:S(2)}) copy-start(bf16[2,896,512]{2,1,0:T(8,128)(2,1)} %wu_ref.3) | copy-start | bytes 5505028
  33.8 21.8 %copy-start = (bf16[2,896,512]{2,1,0:T(8,128)(2,1)S(1)}, bf16[2,896,512]{2,1,0:T(8,128)(2,1)}, u32[]{:S(2)}) copy-start(bf16[2,896,512]{2,1,0:T(8,128)(2,1)} %wg_ref.3) | copy-start | bytes 5505028
  33.8 21.8 %copy-start.4 = (bf16[192,192]{1,0:T(8,128)(2,1)S(1)}, bf16[192,192]{1,0:T(8,128)(2,1)}, u32[]{:S(2)}) copy-start(bf16[192,192]{1,0:T(8,128)(2,1)} %constant.15.clone.perm_ref) | copy-start | bytes 221188
  91.4 23.2 %copy-start.3 = (bf16[192,192]{1,0:T(8,128)(2,1)S(1)}, bf16[192,192]{1,0:T(8,128)(2,1)}, u32[]{:S(2)}) copy-start(bf16[192,192]{1,0:T(8,128)(2,1)} %constant.16.clone.back_ref) | copy-start | bytes 221188
  131.8 13.9 %copy-start.5 = (s32[128,8]{0,1:T(8,128)S(1)}, s32[128,8]{0,1:T(8,128)}, u32[]{:S(2)}) copy-start(s32[128,8]{0,1:T(8,128)} %param.12) | copy-start | bytes 12292

commit v4 on v3

--- a/solution.py
+++ b/solution.py
@@ -178,12 +178,30 @@
     return run
 
 
-def send_whole(packed):
-    return lax.all_to_all(packed, "y", split_axis=0, concat_axis=0, tiled=True)
-
-
-def send_in_pieces(packed):
-    return jnp.concatenate([send_whole(packed[:, :8]), send_whole(packed[:, 8:])], axis=1)
+def exchange(value, axis):
+    return lax.all_to_all(value, axis, split_axis=0, concat_axis=0, tiled=True)
+
+
+def copies_of(packed):
+    count, width = YS * ROWS, packed.shape[2]
+    shape = jax.ShapeDtypeStruct((XS, count, width), BF16)
+    return call(copies_kernel, shape)(packed.reshape(count, width))
+
+
+def dispatch_in_steps(packed):
+    return exchange(copies_of(exchange(packed, "y")), "x")
+
+
+def dispatch_at_once(packed):
+    copies = copies_of(packed).reshape(XS * YS, ROWS, packed.shape[2])
+    return exchange(copies, ("x", "y")).reshape(XS, YS * ROWS, packed.shape[2])
+
+
+def products(rows, chunks, perm, w_gate, w_up, w_down):
+    block, part = YS * CAP, rows.shape[2]
+    return call(first_kernel, chunks, [pltpu.VMEM((4, XS * block, part), BF16)], 24)(
+        perm, rows, w_gate, w_up, w_down
+    )
 
 
 def on_device(tokens, route_cot, expert_ids, w_gate, w_up, w_down):
@@ -208,19 +226,16 @@
         vmem=60,
         space=pltpu.HBM,
     )(ids_t, tokens, route_cot)
-    sliced = lax.cond(
-        lax.rem(lax.axis_index("node"), 2) == 0, send_in_pieces, send_whole, packed
-    )
-    rows = lax.all_to_all(
-        call(copies_kernel, shape((XS, YS * ROWS, part), BF16))(sliced.reshape(YS * ROWS, part)),
-        "x",
-        split_axis=0,
-        concat_axis=0,
-        tiled=True,
-    )
     chunks = shape((2 * XS, block, 3 * hidden), BF16)
-    partials = call(first_kernel, chunks, [pltpu.VMEM((4, XS * block, part), BF16)], 24)(
-        perm, rows, w_gate, w_up, w_down
+    partials = lax.cond(
+        lax.rem(lax.axis_index("node"), 2) == 0,
+        lambda *args: products(dispatch_in_steps(args[0]), chunks, *args[1:]),
+        lambda *args: products(dispatch_at_once(args[0]), chunks, *args[1:]),
+        packed,
+        perm,
+        w_gate,
+        w_up,
+        w_down,
     )
     shares = lax.all_to_all(partials, "y", split_axis=0, concat_axis=0, tiled=True)
     acts = call(act_kernel, chunks)(shares)

time: 147 us -> 136 us (0.925)
  the two profiles are of different devices: /device:TPU:2 before, /device:TPU:960 now
where the time goes in v4:
time: 136 us
  blocking collectives  126 us (93%)
  Pallas kernels  8.3 us (6%)
    all_to_all x2, blocking collectives, exchange(): return lax.all_to_all(value, axis, split_axis=0, concat_axis=0, tiled=True)  38.2 us
    all_to_all x1, blocking collectives, on_device(): lax.all_to_all(partials, 'y', split_axis=0, concat_axis=0, tiled=True)  30.3 us
    all_to_all x1, blocking collectives, on_device(): acts = lax.all_to_all(acts, 'y', split_axis=0, concat_axis=0, tiled=True)  28.7 us
    all_to_all x1, blocking collectives, on_device(): lax.all_to_all(results, 'x', split_axis=0, concat_axis=0, tiled=True)  15.1 us
    all_to_all x1, blocking collectives, on_device(): lax.all_to_all(total.reshape(YS, ROWS, part), 'y', split_axis=0, concat_a...  14.2 us
    pallas_call x7, Pallas kernels, run(): pl.pallas_call(kernel, out_shape=outs, in_specs=[pl.BlockSpec(memory_spac...  8.3 us

profile of v4, /device:TPU:960, one launch (start us, length us, event | category | flops | bytes accessed | tf_op | source)
XLA Modules:
  0.0 135.5 jit_solution(5002025752697390125)
XLA Ops:
  0.6 0.0 copy-start.9
  0.6 0.0 copy-start.2
  0.7 2.4 %shard_map.95 = bf16[8,24,896]{2,1,0:T(8,128)(2,1)S(1)} custom-call(s32[8,128]{1,0:T(8,128)} %bitcast.10, bf16[128,7168]{1,0:T(8,128)(2,1)} %tok_any.1, bf16[12,7168]{1,0:T(8,128)(2,1)} %cot_any.1), custom_call_target="tpu_custom_call" | custom-call | tf_op jit(solution)/shard_map/pallas_call | solution.py:169
  3.1 0.0 copy-done.9
  3.1 0.0 copy-done.2
  3.1 40.3 %conditional.1 = (bf16[8,48,1536]{2,1,0:T(8,128)(2,1)S(1)}) conditional(s32[]{:T(128)} %convert_element_type.3, (bf16[8,24,896]{2,1,0:T(8,128)(2,1)S(1)}, bf16[192,192]{1,0:T(8,128)(2,1)S(1)}, bf16[2,896,512]{2,1,0:T(8,128)(2,1)S(1)}, bf16[2,896,512]{2,1,0:T(8,128)(2,1)}, bf16[2,512,896]{2,1,0:T(8,128)(2,1)}) %tuple.18, ...), branch_computations={%region_0.0_spmd, %region_1.0_spmd} | conditional | bytes 18120768 | solution.py:230
  3.1 20.1 %all_to_all.33 = bf16[8,24,896]{2,1,0:T(8,128)(2,1)S(1)} all-to-all(bf16[8,24,896]{2,1,0:T(8,128)(2,1)S(1)} %get-tuple-element.29), channel_id=1, replica_groups=mesh['node'=32,'x'=4,'y'=8] {'y'}, dimensions={0} | all-to-all | bytes 688128 | tf_op jit(solution)/shard_map/cond/branch_1_fun/all_to_all | solution.py:182
  23.2 0.0 copy-start.8
  23.2 0.1 branch_1_fun.2
  23.4 0.0 copy-start.5
  23.4 18.0 %all_to_all.34.rows_ref = bf16[4,192,896]{2,1,0:T(8,128)(2,1)S(1)} all-to-all(bf16[4,192,896]{2,1,0:T(8,128)(2,1)S(1)} %branch_1_fun.2), channel_id=1, replica_groups=mesh['node'=32,'x'=4,'y'=8] {'x'}, dimensions={0} | all-to-all | bytes 2752512 | tf_op jit(solution)/shard_map/cond/branch_1_fun/all_to_all | solution.py:182
  41.4 0.0 copy-done.8
  41.4 0.0 copy-done.5
  41.4 2.0 %branch_1_fun.3 = bf16[8,48,1536]{2,1,0:T(8,128)(2,1)S(1)} custom-call(bf16[192,192]{1,0:T(8,128)(2,1)S(1)} %get-tuple-element.28.perm_ref, bf16[4,192,896]{2,1,0:T(8,128)(2,1)S(1)} %all_to_all.34.rows_ref, bf16[2,896,512]{2,1,0:T(8,128)(2,1)S(1)} %get-tuple-element.30.wg_ref, bf16[2,896,512]{2,1,0:T(8,128)(2,1)S(1)} %copy-done.5, ...), custom_call_target="tpu_custom_call" | custom-call | tf_op jit(solution)/shard_map/cond/branch_1_fun/pallas_call | solution.py:169
  43.4 30.3 %all_to_all.35.parts_ref = bf16[8,48,1536]{2,1,0:T(8,128)(2,1)S(1)} all-to-all(bf16[8,48,1536]{2,1,0:T(8,128)(2,1)S(1)} %get-tuple-element.35), channel_id=1, replica_groups=mesh['node'=32,'x'=4,'y'=8] {'y'}, dimensions={0} | all-to-all | bytes 2359296 | tf_op jit(solution)/shard_map/all_to_all | solution.py:240
  73.7 0.0 copy-start.6
  73.7 0.2 shard_map.96
  73.9 0.0 copy-start
  73.9 0.0 copy-start.3
  73.9 28.7 %all_to_all.36.act_ref = bf16[8,48,1536]{2,1,0:T(8,128)(2,1)S(1)} all-to-all(bf16[8,48,1536]{2,1,0:T(8,128)(2,1)S(1)} %shard_map.96), channel_id=1, replica_groups=mesh['node'=32,'x'=4,'y'=8] {'y'}, dimensions={0} | all-to-all | bytes 2359296 | tf_op jit(solution)/shard_map/all_to_all | solution.py:242
  102.6 0.0 copy-done.6
  102.6 0.0 copy-done
  102.6 0.0 copy-done.3
  102.6 2.2 %shard_map.97 = bf16[4,192,896]{2,1,0:T(8,128)(2,1)S(1)} custom-call(bf16[192,192]{1,0:T(8,128)(2,1)S(1)} %copy-done, bf16[8,48,1536]{2,1,0:T(8,128)(2,1)S(1)} %all_to_all.36.act_ref, bf16[2,896,512]{2,1,0:T(8,128)(2,1)S(1)} %copy-done.2, bf16[2,896,512]{2,1,0:T(8,128)(2,1)S(1)} %copy-done.3, bf16[2,512,896]{2,1,0:T(8,128)(2,1)S(1)} %copy-done.6), custom_call_target="tpu_custom_call" | custom-call | tf_op jit(solution)/shard_map/pallas_call | solution.py:169
  104.8 15.1 %all_to_all.37.parts_ref = bf16[4,192,896]{2,1,0:T(8,128)(2,1)S(1)} all-to-all(bf16[4,192,896]{2,1,0:T(8,128)(2,1)S(1)} %shard_map.97), channel_id=1, replica_groups=mesh['node'=32,'x'=4,'y'=8] {'x'}, dimensions={0} | all-to-all | bytes 2752512 | tf_op jit(solution)/shard_map/all_to_all | solution.py:249
  119.9 0.0 copy-start.1
  119.9 0.2 shard_map.98
  120.1 14.2 %all_to_all.38.rows_ref = bf16[8,24,896]{2,1,0:T(8,128)(2,1)S(1)} all-to-all(bf16[8,24,896]{2,1,0:T(8,128)(2,1)S(1)} %bitcast.8), channel_id=1, replica_groups=mesh['node'=32,'x'=4,'y'=8] {'y'}, dimensions={0} | all-to-all | bytes 688128 | tf_op jit(solution)/shard_map/all_to_all | solution.py:251
  134.3 0.0 copy-done.1
  134.3 1.3 shard_map.99
Async XLA Ops:
  0.6 2.4 %copy-start.9 = (bf16[192,192]{1,0:T(8,128)(2,1)S(1)}, bf16[192,192]{1,0:T(8,128)(2,1)}, u32[]{:S(2)}) copy-start(bf16[192,192]{1,0:T(8,128)(2,1)} %constant.15.clone) | copy-start | bytes 221188
  0.6 2.4 %copy-start.2 = (bf16[2,896,512]{2,1,0:T(8,128)(2,1)S(1)}, bf16[2,896,512]{2,1,0:T(8,128)(2,1)}, u32[]{:S(2)}) copy-start(bf16[2,896,512]{2,1,0:T(8,128)(2,1)} %wg_ref.1) | copy-start | bytes 5505028
  23.2 18.1 %copy-start.8 = (bf16[2,512,896]{2,1,0:T(8,128)(2,1)S(1)}, bf16[2,512,896]{2,1,0:T(8,128)(2,1)}, u32[]{:S(2)}) copy-start(bf16[2,512,896]{2,1,0:T(8,128)(2,1)} %get-tuple-element.32.wd_ref) | copy-start | bytes 5505028 | tf_op jit(solution)/shard_map/cond
  23.4 18.0 %copy-start.5 = (bf16[2,896,512]{2,1,0:T(8,128)(2,1)S(1)}, bf16[2,896,512]{2,1,0:T(8,128)(2,1)}, u32[]{:S(2)}) copy-start(bf16[2,896,512]{2,1,0:T(8,128)(2,1)} %get-tuple-element.31.wu_ref) | copy-start | bytes 5505028 | tf_op jit(solution)/shard_map/cond
  73.7 29.0 %copy-start.6 = (bf16[2,512,896]{2,1,0:T(8,128)(2,1)S(1)}, bf16[2,512,896]{2,1,0:T(8,128)(2,1)}, u32[]{:S(2)}) copy-start(bf16[2,512,896]{2,1,0:T(8,128)(2,1)} %wd_ref.1) | copy-start | bytes 5505028
  73.9 28.7 %copy-start = (bf16[192,192]{1,0:T(8,128)(2,1)S(1)}, bf16[192,192]{1,0:T(8,128)(2,1)}, u32[]{:S(2)}) copy-start(bf16[192,192]{1,0:T(8,128)(2,1)} %constant.16.clone.back_ref) | copy-start | bytes 221188
  73.9 28.7 %copy-start.3 = (bf16[2,896,512]{2,1,0:T(8,128)(2,1)S(1)}, bf16[2,896,512]{2,1,0:T(8,128)(2,1)}, u32[]{:S(2)}) copy-start(bf16[2,896,512]{2,1,0:T(8,128)(2,1)} %wu_ref.1) | copy-start | bytes 5505028
  119.9 14.4 %copy-start.1 = (s32[128,8]{0,1:T(8,128)S(1)}, s32[128,8]{0,1:T(8,128)}, u32[]{:S(2)}) copy-start(s32[128,8]{0,1:T(8,128)} %param.12) | copy-start | bytes 12292

commit v5 on v4

--- a/solution.py
+++ b/solution.py
@@ -228,7 +228,7 @@
     )(ids_t, tokens, route_cot)
     chunks = shape((2 * XS, block, 3 * hidden), BF16)
     partials = lax.cond(
-        lax.rem(lax.axis_index("node"), 2) == 0,
+        lax.rem(lax.axis_index("node"), 2) == 1,
         lambda *args: products(dispatch_in_steps(args[0]), chunks, *args[1:]),
         lambda *args: products(dispatch_at_once(args[0]), chunks, *args[1:]),
         packed,

time: 136 us -> 150 us (1.10)
  blocking collectives: 126 us -> 141 us
    all_to_all x1, blocking collectives: 28.7 us -> 35.4 us  [on_device(): acts = lax.all_to_all(acts, 'y', split_axis=0, concat_axis=0, tiled=True)]
    all_to_all x1, blocking collectives: 15.1 us -> 21.6 us  [on_device(): lax.all_to_all(results, 'x', split_axis=0, concat_axis=0, tiled=True)]
    all_to_all x2 -> x1, blocking collectives: 38.2 us -> 32.5 us  [exchange(): return lax.all_to_all(value, axis, split_axis=0, concat_axis=0, tiled=True)]
    all_to_all x1, blocking collectives: 30.3 us -> 35.6 us  [on_device(): lax.all_to_all(partials, 'y', split_axis=0, concat_axis=0, tiled=True)]
where the time goes in v5:
time: 150 us
  blocking collectives  141 us (94%)
  Pallas kernels  8.31 us (6%)
    all_to_all x1, blocking collectives, on_device(): lax.all_to_all(partials, 'y', split_axis=0, concat_axis=0, tiled=True)  35.6 us
    all_to_all x1, blocking collectives, on_device(): acts = lax.all_to_all(acts, 'y', split_axis=0, concat_axis=0, tiled=True)  35.4 us
    all_to_all x1, blocking collectives, exchange(): return lax.all_to_all(value, axis, split_axis=0, concat_axis=0, tiled=True)  32.5 us
    all_to_all x1, blocking collectives, on_device(): lax.all_to_all(results, 'x', split_axis=0, concat_axis=0, tiled=True)  21.6 us
    all_to_all x1, blocking collectives, on_device(): lax.all_to_all(total.reshape(YS, ROWS, part), 'y', split_axis=0, concat_a...  15.4 us
    pallas_call x7, Pallas kernels, run(): pl.pallas_call(kernel, out_shape=outs, in_specs=[pl.BlockSpec(memory_spac...  8.31 us

profile of v5, /device:TPU:960, one launch (start us, length us, event | category | flops | bytes accessed | tf_op | source)
XLA Modules:
  0.0 149.7 jit_solution(12335344399884811799)
XLA Ops:
  0.6 0.0 copy-start.9
  0.6 0.0 copy-start.2
  0.7 2.4 %shard_map.95 = bf16[8,24,896]{2,1,0:T(8,128)(2,1)S(1)} custom-call(s32[8,128]{1,0:T(8,128)} %bitcast.10, bf16[128,7168]{1,0:T(8,128)(2,1)} %tok_any.1, bf16[12,7168]{1,0:T(8,128)(2,1)} %cot_any.1), custom_call_target="tpu_custom_call" | custom-call | tf_op jit(solution)/shard_map/pallas_call | solution.py:169
  3.1 0.0 copy-done.9
  3.1 0.0 copy-done.2
  3.1 34.7 %conditional.1 = (bf16[8,48,1536]{2,1,0:T(8,128)(2,1)S(1)}) conditional(s32[]{:T(128)} %convert_element_type.3, (bf16[8,24,896]{2,1,0:T(8,128)(2,1)S(1)}, bf16[192,192]{1,0:T(8,128)(2,1)S(1)}, bf16[2,896,512]{2,1,0:T(8,128)(2,1)S(1)}, bf16[2,896,512]{2,1,0:T(8,128)(2,1)}, bf16[2,512,896]{2,1,0:T(8,128)(2,1)}) %tuple.18, ...), branch_computations={%region_0.0_spmd, %region_1.0_spmd} | conditional | bytes 18120768 | solution.py:230
  3.1 0.0 copy-start.7
  3.1 0.1 branch_0_fun.2
  3.2 0.0 copy-start.4
  3.2 32.5 %all_to_all.32 = bf16[32,24,896]{2,1,0:T(8,128)(2,1)S(1)} all-to-all(bf16[32,24,896]{2,1,0:T(8,128)(2,1)S(1)} %bitcast.6), channel_id=1, replica_groups=mesh['node'=32,'x'=4,'y'=8] {'x','y'}, dimensions={0} | all-to-all | bytes 2752512 | tf_op jit(solution)/shard_map/cond/branch_0_fun/all_to_all | solution.py:182
  35.8 0.0 copy-done.7
  35.8 0.0 copy-done.4
  35.8 2.0 %branch_0_fun.3 = bf16[8,48,1536]{2,1,0:T(8,128)(2,1)S(1)} custom-call(bf16[192,192]{1,0:T(8,128)(2,1)S(1)} %get-tuple-element.14.perm_ref, bf16[4,192,896]{2,1,0:T(8,128)(2,1)S(1)} %bitcast.7, bf16[2,896,512]{2,1,0:T(8,128)(2,1)S(1)} %get-tuple-element.25.wg_ref, bf16[2,896,512]{2,1,0:T(8,128)(2,1)S(1)} %copy-done.4, bf16[2,512,896]{2,1,0:T(8,128)(2,1)S(1)} %copy-done.7), custom_call_target="tpu_custom_call" | custom-call | tf_op jit(solution)/shard_map/cond/branch_0_fun/pallas_call | solution.py:169
  37.8 35.6 %all_to_all.35.parts_ref = bf16[8,48,1536]{2,1,0:T(8,128)(2,1)S(1)} all-to-all(bf16[8,48,1536]{2,1,0:T(8,128)(2,1)S(1)} %get-tuple-element.35), channel_id=1, replica_groups=mesh['node'=32,'x'=4,'y'=8] {'y'}, dimensions={0} | all-to-all | bytes 2359296 | tf_op jit(solution)/shard_map/all_to_all | solution.py:240
  73.4 0.0 copy-start.6
  73.4 0.2 shard_map.96
  73.6 0.0 copy-start
  73.6 0.0 copy-start.3
  73.6 35.4 %all_to_all.36.act_ref = bf16[8,48,1536]{2,1,0:T(8,128)(2,1)S(1)} all-to-all(bf16[8,48,1536]{2,1,0:T(8,128)(2,1)S(1)} %shard_map.96), channel_id=1, replica_groups=mesh['node'=32,'x'=4,'y'=8] {'y'}, dimensions={0} | all-to-all | bytes 2359296 | tf_op jit(solution)/shard_map/all_to_all | solution.py:242
  109.0 0.0 copy-done.6
  109.0 0.0 copy-done
  109.0 0.0 copy-done.3
  109.1 2.2 %shard_map.97 = bf16[4,192,896]{2,1,0:T(8,128)(2,1)S(1)} custom-call(bf16[192,192]{1,0:T(8,128)(2,1)S(1)} %copy-done, bf16[8,48,1536]{2,1,0:T(8,128)(2,1)S(1)} %all_to_all.36.act_ref, bf16[2,896,512]{2,1,0:T(8,128)(2,1)S(1)} %copy-done.2, bf16[2,896,512]{2,1,0:T(8,128)(2,1)S(1)} %copy-done.3, bf16[2,512,896]{2,1,0:T(8,128)(2,1)S(1)} %copy-done.6), custom_call_target="tpu_custom_call" | custom-call | tf_op jit(solution)/shard_map/pallas_call | solution.py:169
  111.2 21.6 %all_to_all.37.parts_ref = bf16[4,192,896]{2,1,0:T(8,128)(2,1)S(1)} all-to-all(bf16[4,192,896]{2,1,0:T(8,128)(2,1)S(1)} %shard_map.97), channel_id=1, replica_groups=mesh['node'=32,'x'=4,'y'=8] {'x'}, dimensions={0} | all-to-all | bytes 2752512 | tf_op jit(solution)/shard_map/all_to_all | solution.py:249
  132.8 0.0 copy-start.1
  132.8 0.2 shard_map.98
  133.0 15.4 %all_to_all.38.rows_ref = bf16[8,24,896]{2,1,0:T(8,128)(2,1)S(1)} all-to-all(bf16[8,24,896]{2,1,0:T(8,128)(2,1)S(1)} %bitcast.8), channel_id=1, replica_groups=mesh['node'=32,'x'=4,'y'=8] {'y'}, dimensions={0} | all-to-all | bytes 688128 | tf_op jit(solution)/shard_map/all_to_all | solution.py:251
  148.4 0.0 copy-done.1
  148.4 1.3 shard_map.99
Async XLA Ops:
  0.6 2.4 %copy-start.9 = (bf16[192,192]{1,0:T(8,128)(2,1)S(1)}, bf16[192,192]{1,0:T(8,128)(2,1)}, u32[]{:S(2)}) copy-start(bf16[192,192]{1,0:T(8,128)(2,1)} %constant.15.clone) | copy-start | bytes 221188
  0.6 2.4 %copy-start.2 = (bf16[2,896,512]{2,1,0:T(8,128)(2,1)S(1)}, bf16[2,896,512]{2,1,0:T(8,128)(2,1)}, u32[]{:S(2)}) copy-start(bf16[2,896,512]{2,1,0:T(8,128)(2,1)} %wg_ref.1) | copy-start | bytes 5505028
  3.1 32.7 %copy-start.7 = (bf16[2,512,896]{2,1,0:T(8,128)(2,1)S(1)}, bf16[2,512,896]{2,1,0:T(8,128)(2,1)}, u32[]{:S(2)}) copy-start(bf16[2,512,896]{2,1,0:T(8,128)(2,1)} %get-tuple-element.27.wd_ref) | copy-start | bytes 5505028 | tf_op jit(solution)/shard_map/cond
  3.2 32.6 %copy-start.4 = (bf16[2,896,512]{2,1,0:T(8,128)(2,1)S(1)}, bf16[2,896,512]{2,1,0:T(8,128)(2,1)}, u32[]{:S(2)}) copy-start(bf16[2,896,512]{2,1,0:T(8,128)(2,1)} %get-tuple-element.26.wu_ref) | copy-start | bytes 5505028 | tf_op jit(solution)/shard_map/cond
  73.4 35.7 %copy-start.6 = (bf16[2,512,896]{2,1,0:T(8,128)(2,1)S(1)}, bf16[2,512,896]{2,1,0:T(8,128)(2,1)}, u32[]{:S(2)}) copy-start(bf16[2,512,896]{2,1,0:T(8,128)(2,1)} %wd_ref.1) | copy-start | bytes 5505028
  73.6 35.4 %copy-start = (bf16[192,192]{1,0:T(8,128)(2,1)S(1)}, bf16[192,192]{1,0:T(8,128)(2,1)}, u32[]{:S(2)}) copy-start(bf16[192,192]{1,0:T(8,128)(2,1)} %constant.16.clone.back_ref) | copy-start | bytes 221188
  73.6 35.4 %copy-start.3 = (bf16[2,896,512]{2,1,0:T(8,128)(2,1)S(1)}, bf16[2,896,512]{2,1,0:T(8,128)(2,1)}, u32[]{:S(2)}) copy-start(bf16[2,896,512]{2,1,0:T(8,128)(2,1)} %wu_ref.1) | copy-start | bytes 5505028
  132.8 15.6 %copy-start.1 = (s32[128,8]{0,1:T(8,128)S(1)}, s32[128,8]{0,1:T(8,128)}, u32[]{:S(2)}) copy-start(s32[128,8]{0,1:T(8,128)} %param.12) | copy-start | bytes 12292
